TPU v7x, 256 devices: a whole 4x4x8 slice. The times are simulated.
256 devices in a mesh: dp: 64 (over y, z, core), hidden: 4 (over x).
Axes of the slice: x: 4, y: 4, z: 8, core: 2. Of those that a mesh axis runs over, the one named last changes fastest.
Arguments:
- tokens: bfloat16 [32768, 8192], P('dp', 'hidden'), may hold values from -6 to 6
- qkv_weight: float32 [5120, 8192], P('dp', 'hidden'), may hold values from -24 to 24
- grad: float32 [5120, 8192], P('dp', 'hidden'), may hold values from -6 to 6
- adam_m: float32 [5120, 8192], P('dp', 'hidden'), may hold values from -2 to 2
- adam_v: float32 [5120, 8192], P('dp', 'hidden'), may hold values from 0.05 to 1
- head_gain: float32 [5120], P('hidden'), may hold values from 0.25 to 1.75
Outputs:
- new_weight: float32 [5120, 8192], P('dp', 'hidden')
- new_m: float32 [5120, 8192], P('dp', 'hidden')
- new_v: float32 [5120, 8192], P('dp', 'hidden')
- qkv: bfloat16 [32768, 5120], P('dp', 'hidden')
All inputs are finite; a program needn't handle non-finite values.
Results may differ from a plain program's by a relative error of at most 0.015.
Values may be sent and summed in bfloat16 or wider, within the bound.
A program may use at most 192 MiB of HBM per device.

v0:
```python
import math

import jax
import jax.numpy as jnp
from jax import lax
from jax.sharding import PartitionSpec as P

D = 8192
HD = 128
QR = 4096
KR = 512


beta_one = 0.9
beta_two = 0.95
learn_rate = 0.05
adam_eps = 1e-08
norm_eps = 1e-06
bias_one = 0.999973438601112
bias_two = 0.994079470779667


def body(tokens, qkv_weight, grad, adam_m, adam_v, head_gain):
    new_m = beta_one * adam_m + (1.0 - beta_one) * grad
    new_v = beta_two * adam_v + (1.0 - beta_two) * grad * grad
    updated = qkv_weight - learn_rate * (new_m / bias_one) / (jnp.sqrt(new_v / bias_two) + adam_eps)
    partial_value = jnp.sum(updated * updated, axis=1)
    weight_bf = updated.astype(jnp.bfloat16)
    row_total = lax.psum(partial_value, "hidden")
    row_scale = 1.0 / jnp.sqrt(row_total / D + norm_eps)
    all_scale = lax.all_gather(row_scale, "dp", axis=0, tiled=True)
    new_weight = updated * row_scale[:, None]
    tok_rows = tokens.shape[0]
    local_cols = head_gain.shape[0]
    col_start = lax.axis_index("hidden") * local_cols
    partial_proj = lax.dot_general(
        tokens,
        lax.all_gather(weight_bf, "dp", axis=0, tiled=True),
        (((1,), (1,)), ((), ())),
        preferred_element_type=jnp.float32,
    )
    summed = lax.psum_scatter(
        partial_proj.astype(jnp.bfloat16), "hidden", scatter_dimension=1, tiled=True
    ).astype(jnp.float32)
    col_scale = lax.dynamic_slice_in_dim(all_scale, col_start, local_cols, 0)
    proj = summed * col_scale[None, :]
    heads = proj.reshape(tok_rows, local_cols // HD, HD)
    mean_sq = jnp.mean(heads * heads, axis=2, keepdims=True)
    normed = heads / jnp.sqrt(mean_sq + norm_eps)
    plain = heads / math.sqrt(D)
    head_index = col_start // HD + jnp.arange(local_cols // HD, dtype=jnp.int32)
    is_qk = (head_index < (QR + KR) // HD)[None, :, None]
    result = jnp.where(is_qk, normed, plain).reshape(tok_rows, local_cols) * head_gain[None, :]
    return (new_weight, new_m, new_v, result.astype(jnp.bfloat16))


def solution(mesh):
    return jax.shard_map(
        body,
        mesh=mesh,
        in_specs=(
            P("dp", "hidden"),
            P("dp", "hidden"),
            P("dp", "hidden"),
            P("dp", "hidden"),
            P("dp", "hidden"),
            P("hidden"),
        ),
        out_specs=(P("dp", "hidden"), P("dp", "hidden"), P("dp", "hidden"), P("dp", "hidden")),
        check_vma=False,
    )
```

profile of v0, /device:TPU:1, one launch (start us, length us, event | category | flops | bytes accessed | tf_op | source)
XLA Modules:
  0.0 413.0 jit_solution(7113517782043175637)
XLA Ops:
  7.2 0.0 copy-start
  7.2 0.0 all-gather.2.cloned.1.call-start
  7.2 3.2 fusion.7
  10.5 0.0 all-gather.2.cloned.1.call-update
  10.5 0.0 reduce-scatter.2.cloned.1.call-start
  10.5 115.6 %all-gather.2.cloned.1.call-done = bf16[5120,2048]{1,0:T(8,128)(2,1)} async-done(((bf16[80,2048]{1,0:T(8,128)(2,1)}), bf16[5120,2048]{1,0:T(8,128)(2,1)}) %all-gather.2.cloned.1.call-update) | async-done | bytes 20971536 | tf_op jit(solution)/shard_map/all_gather | solution.py:38
  126.2 0.0 copy-done
  126.2 16.8 %fusion = bf16[512,5120]{0,1:T(8,128)(2,1)} fusion(bf16[5120,2048]{1,0:T(8,128)(2,1)} %all-gather.2.cloned.1.call-done, bf16[512,2048]{1,0:T(8,128)(2,1)S(1)} %copy-done), kind=kOutput, calls=%fused_computation.1 | convolution fusion | flops 10740039680 | bytes 28311552 | tf_op jit(solution)/shard_map/dot_general | solution.py:36
  143.0 0.0 copy-start.2
  143.0 0.0 reduce-scatter.2.cloned.1.call-update
  143.1 0.6 copy-done.2
  143.7 0.6 dynamic-slice
  144.9 0.1 multiply_reduce_fusion
  145.1 8.4 %psum.7 = f32[80]{0:T(128)S(1)} all-reduce(f32[80]{0:T(128)S(1)} %multiply_reduce_fusion), channel_id=1, replica_groups=mesh['dp'=64,'hidden'=4] {'hidden'}, use_global_device_ids=true, to_apply=%region_1.0 | all-reduce | flops 80 | bytes 640 | tf_op jit(solution)/shard_map/psum | solution.py:29
  153.5 0.1 fusion.6
  153.6 242.8 %all-reduce = f32[5120]{0:T(1024)S(1)} all-reduce(f32[5120]{0:T(1024)S(1)} %get-tuple-element.12), channel_id=1, replica_groups=mesh['dp'=64,'hidden'=4] {'dp'}, use_global_device_ids=true, to_apply=%add | all-reduce | flops 5120 | bytes 40960
  396.4 0.1 dynamic_slice.3
  396.5 0.1 broadcast_bitcast_fusion
  396.5 0.9 broadcast_multiply_fusion
  397.5 0.0 copy-start.1
  397.5 0.0 reduce-scatter.2.cloned.1.call-done
  397.5 3.2 fusion.4
  400.6 2.0 reduce_sum.19
  402.7 0.0 copy-done.1
  402.7 2.0 fusion.3
  404.7 1.4 copy.10
  (3 shorter events, 0.0 us)
Async XLA Ops:
  7.2 119.0 %copy-start = (bf16[512,2048]{1,0:T(8,128)(2,1)S(1)}, bf16[512,2048]{1,0:T(8,128)(2,1)}, u32[]{:S(2)}) copy-start(bf16[512,2048]{1,0:T(8,128)(2,1)} %param.6) | copy-start | bytes 6291460
  7.2 119.0 %all-gather.2.cloned.1.call-start = ((), (), s32[]{:S(2)}) async-start(), calls=%async_computation.1 | async-start | bytes 21299200 | tf_op jit(solution)/shard_map/all_gather | solution.py:38
  10.5 387.0 %reduce-scatter.2.cloned.1.call-start = ((), (), s32[]{:S(2)}) async-start(), calls=%async_computation.2 | async-start | bytes 6553600 | tf_op jit(solution)/shard_map/reduce_scatter | solution.py:42
  143.0 0.7 copy-start.2
  397.5 5.2 %copy-start.1 = (f32[1280]{0:T(1024)S(1)}, f32[1280]{0:T(1024)}, u32[]{:S(2)}) copy-start(f32[1280]{0:T(1024)} %param.11) | copy-start | bytes 15364
Sparse Core Ops, SparseCore 0:
  11.3 114.8 all-gather.1
  143.2 54.5 reduce-scatter.1
where the time goes:
time: 416 us; the launch traced here: 413 us
  blocking collectives  251 us (60%)
  waiting for transfers between devices  116 us (28%)
  matrix products  16.8 us (4%)
  between operations  14.7 us (4%)
  other arithmetic  11.6 us (3%)
    unnamed x1, blocking collectives  243 us
    all_gather x1, waiting for transfers between devices, body(): lax.all_gather(weight_bf, 'dp', axis=0, tiled=True)  116 us
    dot_general x1, matrix products, body(): lax.dot_general(tokens, lax.all_gather(weight_bf, 'dp', axis=0, tiled=Tru...  16.8 us
    psum x1, blocking collectives, body(): row_total = lax.psum(partial_value, 'hidden')  8.4 us
  transfers between devices with their start and end apart: 2, of which 1 were waited for; matrix products, arithmetic and copies ran while one was open for 0% of the time, Pallas kernels for 0%

commit v1 on v0

--- a/solution.py
+++ b/solution.py
@@ -28,21 +28,25 @@
     weight_bf = updated.astype(jnp.bfloat16)
     row_total = lax.psum(partial_value, "hidden")
     row_scale = 1.0 / jnp.sqrt(row_total / D + norm_eps)
-    all_scale = lax.all_gather(row_scale, "dp", axis=0, tiled=True)
     new_weight = updated * row_scale[:, None]
     tok_rows = tokens.shape[0]
     local_cols = head_gain.shape[0]
     col_start = lax.axis_index("hidden") * local_cols
+    gathered = lax.all_gather(weight_bf, "dp", axis=0, tiled=True)
+    wide = gathered.astype(jnp.float32)
+    col_total = lax.psum_scatter(
+        jnp.sum(wide * wide, axis=1), "hidden", scatter_dimension=0, tiled=True
+    )
+    col_scale = 1.0 / jnp.sqrt(col_total / D + norm_eps)
     partial_proj = lax.dot_general(
         tokens,
-        lax.all_gather(weight_bf, "dp", axis=0, tiled=True),
+        gathered,
         (((1,), (1,)), ((), ())),
         preferred_element_type=jnp.float32,
     )
     summed = lax.psum_scatter(
         partial_proj.astype(jnp.bfloat16), "hidden", scatter_dimension=1, tiled=True
     ).astype(jnp.float32)
-    col_scale = lax.dynamic_slice_in_dim(all_scale, col_start, local_cols, 0)
     proj = summed * col_scale[None, :]
     heads = proj.reshape(tok_rows, local_cols // HD, HD)
     mean_sq = jnp.mean(heads * heads, axis=2, keepdims=True)

time: 416 us -> 214 us (0.51)
  blocking collectives: 251 us -> 15.4 us
  waiting for transfers between devices: 116 us -> 143 us
  other arithmetic: 11.6 us -> 21 us
    unnamed x1 -> x0, blocking collectives: 243 us -> none
    reduce_scatter x1, waiting for transfers between devices: 0.01 us -> 27.3 us  [body(): lax.psum_scatter(partial_proj.astype(jnp.bfloat16), 'hidden', scatter_dim...]
    reduce_sum x0 -> x1, other arithmetic: none -> 9.34 us  [body(): jnp.sum(wide * wide, axis=1)]
    psum x1, blocking collectives: 8.4 us -> 15.4 us  [body(): row_total = lax.psum(partial_value, 'hidden')]
  transfers between devices with their start and end apart: 2 -> 2, of which waited for: 1 -> 2; matrix products, arithmetic and copies ran while one was open for 0% -> 5% of each run, Pallas kernels for 0% -> 0%
where the time goes in v1:
time: 214 us
  waiting for transfers between devices  143 us (67%)
  other arithmetic  21 us (10%)
  matrix products  16.8 us (8%)
  blocking collectives  15.4 us (7%)
  between operations  14.8 us (7%)
  local copies, waits for them, and re-layouts  2.75 us (1%)
    all_gather x1, waiting for transfers between devices, body(): gathered = lax.all_gather(weight_bf, 'dp', axis=0, tiled=True)  116 us
    reduce_scatter x1, waiting for transfers between devices, body(): lax.psum_scatter(partial_proj.astype(jnp.bfloat16), 'hidden', scatter_dim...  27.3 us
    dot_general x1, matrix products, body(): lax.dot_general(tokens, gathered, (((1,), (1,)), ((), ())), preferred_ele...  16.8 us
    psum x1, blocking collectives, body(): row_total = lax.psum(partial_value, 'hidden')  15.4 us
    reduce_sum x1, other arithmetic, body(): jnp.sum(wide * wide, axis=1)  9.34 us
  transfers between devices with their start and end apart: 2, of which 2 were waited for; matrix products, arithmetic and copies ran while one was open for 5% of the time, Pallas kernels for 0%

profile of v1, /device:TPU:1, one launch (start us, length us, event | category | flops | bytes accessed | tf_op | source)
XLA Modules:
  0.0 213.8 jit_solution(6167708148114457999)
XLA Ops:
  7.2 0.0 copy-start
  7.2 0.0 all-gather.2.cloned.1.call-start
  7.2 3.2 %fusion.8 = (bf16[80,2048]{1,0:T(8,128)(2,1)}, f32[80,2048]{1,0:T(8,128)S(1)}, f32[80,2048]{1,0:T(8,128)}, f32[80,2048]{1,0:T(8,128)}) fusion(f32[80,2048]{1,0:T(8,128)} %param.7, f32[80,2048]{1,0:T(8,128)} %param.8, f32[80,2048]{1,0:T(8,128)} %param.9, f32[80,2048]{1,0:T(8,128)} %param.10), kind=kLoop, calls=%fused_computation.22 | loop fusion | flops 2129920 | bytes 4915200 | tf_op jit(solution)/shard_map/convert_element_type | solution.py:28
  10.5 0.0 all-gather.2.cloned.1.call-update
  10.5 0.0 reduce-scatter.2.cloned.1.call-start
  10.5 115.6 %all-gather.2.cloned.1.call-done = bf16[5120,2048]{1,0:T(8,128)(2,1)} async-done(((bf16[80,2048]{1,0:T(8,128)(2,1)}), bf16[5120,2048]{1,0:T(8,128)(2,1)}) %all-gather.2.cloned.1.call-update) | async-done | bytes 20971536 | tf_op jit(solution)/shard_map/all_gather | solution.py:35
  126.2 0.0 copy-done
  126.2 16.8 %fusion = bf16[512,5120]{0,1:T(8,128)(2,1)} fusion(bf16[5120,2048]{1,0:T(8,128)(2,1)} %all-gather.2.cloned.1.call-done, bf16[512,2048]{1,0:T(8,128)(2,1)S(1)} %copy-done), kind=kOutput, calls=%fused_computation.2 | convolution fusion | flops 10740039680 | bytes 28311552 | tf_op jit(solution)/shard_map/dot_general | solution.py:41
  143.0 0.0 copy-start.2
  143.0 0.0 reduce-scatter.2.cloned.1.call-update
  143.1 0.6 copy-done.2
  143.7 0.6 dynamic-slice
  145.0 0.1 multiply_reduce_fusion.1
  145.1 0.1 broadcast_bitcast_fusion
  145.2 9.3 %multiply_reduce_fusion = f32[5120]{0:T(1024)S(1)} fusion(bf16[5120,2048]{1,0:T(8,128)(2,1)} %all-gather.2.cloned.1.call-done), kind=kLoop, calls=%fused_computation | loop fusion | flops 31452160 | bytes 20992000 | tf_op jit(solution)/shard_map/reduce_sum | solution.py:38
  154.5 15.4 %all-reduce.1 = (f32[80]{0:T(128)S(1)}, f32[5120]{0:T(1024)S(1)}) all-reduce(f32[80]{0:T(128)S(1)} %multiply_reduce_fusion.1, f32[5120]{0:T(1024)S(1)} %multiply_reduce_fusion), channel_id=1, replica_groups=mesh['dp'=64,'hidden'=4] {'hidden'}, use_global_device_ids=true, to_apply=%region_1.0 | all-reduce | flops 5200 | bytes 41600 | tf_op jit(solution)/shard_map/psum | solution.py:29
  170.0 0.1 fusion.7
  170.0 1.0 broadcast_multiply_fusion
  171.0 0.0 copy-start.1
  171.0 27.3 %reduce-scatter.2.cloned.1.call-done = bf16[512,1280]{0,1:T(8,128)(2,1)} async-done(((bf16[512,5120]{0,1:T(8,128)(2,1)}), bf16[512,1280]{0,1:T(8,128)(2,1)}) %reduce-scatter.2.cloned.1.call-update) | async-done | bytes 1310736 | tf_op jit(solution)/shard_map/reduce_scatter | solution.py:47
  198.3 3.1 %fusion.4 = f32[512,1280]{0,1:T(8,128)} fusion(bf16[512,1280]{0,1:T(8,128)(2,1)} %reduce-scatter.2.cloned.1.call-done, f32[1280]{0:T(1024)S(1)} %fusion.7), kind=kLoop, calls=%fused_computation.8 | loop fusion | flops 1966080 | bytes 3937280 | tf_op jit(solution)/shard_map/mul | solution.py:52
  201.5 2.0 reduce_sum.29
  203.5 0.0 copy-done.1
  203.6 2.0 fusion.3
  205.5 1.4 copy.11
  (3 shorter events, 0.0 us)
Async XLA Ops:
  7.2 119.0 %copy-start = (bf16[512,2048]{1,0:T(8,128)(2,1)S(1)}, bf16[512,2048]{1,0:T(8,128)(2,1)}, u32[]{:S(2)}) copy-start(bf16[512,2048]{1,0:T(8,128)(2,1)} %param.6) | copy-start | bytes 6291460
  7.2 119.0 %all-gather.2.cloned.1.call-start = ((), (), s32[]{:S(2)}) async-start(), calls=%async_computation.1 | async-start | bytes 21299200 | tf_op jit(solution)/shard_map/all_gather | solution.py:35
  10.5 187.8 %reduce-scatter.2.cloned.1.call-start = ((), (), s32[]{:S(2)}) async-start(), calls=%async_computation.2 | async-start | bytes 6553600 | tf_op jit(solution)/shard_map/reduce_scatter | solution.py:47
  143.0 0.7 copy-start.2
  171.0 32.5 %copy-start.1 = (f32[1280]{0:T(1024)S(1)}, f32[1280]{0:T(1024)}, u32[]{:S(2)}) copy-start(f32[1280]{0:T(1024)} %param.11) | copy-start | bytes 15364
Sparse Core Ops, SparseCore 0:
  11.3 114.8 all-gather.1
  143.2 55.1 reduce-scatter.1

commit v2 on v0

v2 whole, which is shorter than its diff:
```python
import math

import jax
import jax.numpy as jnp
from jax import lax
from jax.experimental import pallas as pl
from jax.experimental.pallas import tpu as pltpu
from jax.sharding import PartitionSpec as P

D = 8192
HD = 128
QR = 4096
KR = 512

NY, NZ, NX = 4, 8, 4
ROWS = 80
SPLIT = 32
KS = 2048
TOK = 512
COLS = 1280
HALF = KS // 2

beta_one = 0.9
beta_two = 0.95
learn_rate = 0.05
adam_eps = 1e-08
norm_eps = 1e-06
bias_one = 0.999973438601112
bias_two = 0.994079470779667

MESH = pl.DeviceIdType.MESH
SIGNS = (1, -1)


def side(s):
    return 0 if s > 0 else 1


def group_of(dz):
    if dz == 0:
        return 0
    if dz == 4:
        return 7
    return 2 * dz - 1 if dz > 0 else -2 * dz


def kernel(
    tok, upd, gain, out, scale_out,
    wbuf, tokbuf, pbuf, inc, rel, fin, sq,
    s_ay, r_ay, s_az, r_az, s_bz, r_bz, s_by, r_by,
    s_x, r_inc, r_fin, r_sib, s_sq, r_sq, tok_sem,
):
    dp = lax.axis_index("dp")
    x = lax.axis_index("hidden")
    y = lax.div(dp, 16)
    z = lax.rem(lax.div(dp, 2), NZ)
    c = lax.rem(dp, 2)

    def device(dy=0, dz=0, dx=0, core=None):
        yy = lax.rem(y + dy + NY, NY)
        zz = lax.rem(z + dz + NZ, NZ)
        return ((yy * NZ + zz) * 2 + (c if core is None else core), lax.rem(x + dx + NX, NX))

    def at_y(dy):
        return lax.rem(y + dy + NY, NY)

    def at_z(dz):
        return lax.rem(z + dz + NZ, NZ)

    def at_x(dx):
        return lax.rem(x + dx + NX, NX)

    y_dev = {s: device(dy=s) for s in SIGNS}
    z_dev = {s: device(dz=s) for s in SIGNS}
    x_dev = {(s, k): device(dx=s, core=k) for s in SIGNS for k in (0, 1)}
    x_two = device(dx=2)
    sibling = device(core=1 - c)

    barrier = pltpu.get_barrier_semaphore()
    partners = list(y_dev.values()) + list(z_dev.values()) + list(x_dev.values()) + [x_two, sibling]
    for partner in partners:
        pl.semaphore_signal(barrier, inc=1, device_id=partner, device_id_type=MESH)

    def copy(src, dst, send_sem, recv_sem, dev):
        return pltpu.make_async_remote_copy(
            src_ref=src, dst_ref=dst, send_sem=send_sem, recv_sem=recv_sem,
            device_id=dev, device_id_type=MESH,
        )

    own_tok = pltpu.make_async_copy(tok, tokbuf.at[c], tok_sem.at[0])
    own_tok.start()

    updated = upd[...]
    squares = updated * updated
    part = squares[:, 0:128]
    for i in range(1, KS // 128):
        part = part + squares[:, i * 128:(i + 1) * 128]
    sq[x] = part

    pl.semaphore_wait(barrier, len(partners))

    sq_dev = {1: device(dx=1), 2: x_two, 3: device(dx=3)}
    sq_out = [copy(sq.at[x], sq.at[x], s_sq.at[d - 1], r_sq.at[d - 1], sq_dev[d]) for d in (1, 2, 3)]
    for d in (1, 0, 2):
        sq_out[d].start()
    tok_out = copy(tok, tokbuf.at[c], tok_sem.at[1], tok_sem.at[2], sibling)
    tok_out.start()
    for d in (1, 2, 3):
        slot = sq.at[at_x(-d)]
        copy(slot, slot, s_sq.at[d - 1], r_sq.at[d - 1], sibling).wait_recv()
    total = jnp.sum(sq[0] + sq[1] + sq[2] + sq[3], axis=1, keepdims=True)
    row_scale = 1.0 / jnp.sqrt(total / D + norm_eps)
    scale_out[...] = jnp.broadcast_to(row_scale, (ROWS, 128))
    wbuf[z, y] = (updated * row_scale).astype(jnp.bfloat16)

    def part_a(zz, yy, s=None):
        ref = wbuf.at[zz, yy, pl.ds(0, SPLIT)]
        return ref if s is None else ref.at[:, pl.ds(side(s) * HALF, HALF)]

    def part_b(zz, yy, s=None):
        ref = wbuf.at[zz, yy, pl.ds(SPLIT, ROWS - SPLIT)]
        return ref if s is None else ref.at[:, pl.ds(side(s) * HALF, HALF)]

    y_order = (0, -1, 1, 2)

    def ay(hop, s):
        if hop == 1:
            ref = part_a(z, y)
        else:
            ref = part_a(z, at_y(-s), s)
        return copy(ref, ref, s_ay.at[hop - 1, side(s)], r_ay.at[hop - 1, side(s)], y_dev[s])

    def ay_recv(hop, s):
        ref = part_a(z, at_y(-s)) if hop == 1 else part_a(z, at_y(-2 * s), s)
        copy(ref, ref, s_ay.at[hop - 1, side(s)], r_ay.at[hop - 1, side(s)], y_dev[s]).wait_recv()

    def az(k, s, j):
        ref = part_a(at_z(-(k - 1) * s), at_y(y_order[j]), s if k == 4 else None)
        return copy(ref, ref, s_az.at[k - 1, side(s), j], r_az.at[k - 1, side(s), j], z_dev[s])

    def az_recv(k, s, j):
        ref = part_a(at_z(-k * s), at_y(y_order[j]), s if k == 4 else None)
        copy(ref, ref, s_az.at[k - 1, side(s), j], r_az.at[k - 1, side(s), j], z_dev[s]).wait_recv()

    def bz(k, s):
        ref = part_b(at_z(-(k - 1) * s), y, s if k == 4 else None)
        return copy(ref, ref, s_bz.at[k - 1, side(s)], r_bz.at[k - 1, side(s)], z_dev[s])

    def bz_recv(k, s):
        ref = part_b(at_z(-k * s), y, s if k == 4 else None)
        copy(ref, ref, s_bz.at[k - 1, side(s)], r_bz.at[k - 1, side(s)], z_dev[s]).wait_recv()

    def by(dz, hop, s):
        g = group_of(dz)
        ref = part_b(at_z(-dz), y) if hop == 1 else part_b(at_z(-dz), at_y(-s), s)
        return copy(ref, ref, s_by.at[g, hop - 1, side(s)], r_by.at[g, hop - 1, side(s)], y_dev[s])

    def by_recv(dz, hop, s):
        g = group_of(dz)
        ref = part_b(at_z(-dz), at_y(-s)) if hop == 1 else part_b(at_z(-dz), at_y(-2 * s), s)
        copy(ref, ref, s_by.at[g, hop - 1, side(s)], r_by.at[g, hop - 1, side(s)], y_dev[s]).wait_recv()

    for s in SIGNS:
        ay(1, s).start()
        bz(1, s).start()
    for s in SIGNS:
        by(0, 1, s).start()
        az(1, s, 0).start()

    def widen(k):
        for s in SIGNS:
            for j in range(4):
                az_recv(k, s, j)
                az(k + 1, s, j).start()
        widen_b(k + 1)
        for dz in (k, -k):
            for s in SIGNS:
                by_recv(dz, 1, s)
                by(dz, 2, s).start()

    def widen_b(k):
        if k < 4:
            for s in SIGNS:
                bz_recv(k, s)
                bz(k + 1, s).start()
                for t in SIGNS:
                    by(k * s, 1, t).start()
        else:
            for s in SIGNS:
                bz_recv(k, s)
            for t in SIGNS:
                by(4, 1, t).start()

    def arrive(dz):
        for s in SIGNS:
            by_recv(dz, 2, s)

    def step_0():
        for s in SIGNS:
            ay_recv(1, s)
            ay(2, s).start()
        for j in (1, 2):
            for s in SIGNS:
                az(1, s, j).start()
        widen_b(1)
        for s in SIGNS:
            by_recv(0, 1, s)
            by(0, 2, s).start()
        for s in SIGNS:
            ay_recv(2, s)
        for s in SIGNS:
            az(1, s, 3).start()
        arrive(0)

    def step_odd(k):
        def run():
            widen(k)
            arrive(k)
        return run

    def step_even(k):
        return lambda: arrive(-k)

    def step_7():
        for s in SIGNS:
            for j in range(4):
                az_recv(4, s, j)
            by_recv(4, 1, s)
            by(4, 2, s).start()
        arrive(4)

    steps = [step_0, step_odd(1), step_even(1), step_odd(2), step_even(2), step_odd(3), step_even(3), step_7]

    own_tok.wait()
    copy(tok, tokbuf.at[1 - c], tok_sem.at[1], tok_sem.at[2], sibling).wait_recv()

    def z_of(g):
        dz = jnp.where(lax.rem(g, 2) == 1, lax.div(g + 1, 2), -lax.div(g, 2))
        return lax.rem(z - dz + NZ, NZ)

    def place(zz, core):
        return pl.ds(pl.multiple_of(zz * (2 * ROWS) + core * ROWS, 16), ROWS)

    def send(g, i):
        zz = z_of(g)
        here = place(zz, c)
        fin_sem = lambda k: r_fin.at[k, zz, c]
        src, dst, recv_sem, dev = (
            lambda: (pbuf.at[g, at_x(2), 0], inc.at[g, 0], r_inc.at[g, 0], device(dx=-1)),
            lambda: (pbuf.at[g, at_x(2), 1], inc.at[g, 1], r_inc.at[g, 1], device(dx=1)),
            lambda: (pbuf.at[g, at_x(-1), 1], fin.at[0, here], fin_sem(0), x_dev[-1, 1]),
            lambda: (pbuf.at[g, at_x(1), 0], fin.at[1, here], fin_sem(1), x_dev[1, 0]),
            lambda: (pbuf.at[g, x, 1 - c], fin.at[2, here], r_sib.at[zz], sibling),
            lambda: (rel.at[g, 0], fin.at[0, here], fin_sem(0), x_dev[-1, 0]),
            lambda: (rel.at[g, 1], fin.at[1, here], fin_sem(1), x_dev[1, 1]),
        )[i]()
        return copy(src, dst, s_x.at[g, i], recv_sem, dev)

    def relay(g):
        for i, owner in ((0, at_x(-1)), (1, at_x(1))):
            send(g, i).wait_recv()
            mixed = pbuf[g, owner, i].astype(jnp.float32) + inc[g, i].astype(jnp.float32)
            rel[g, i] = mixed.astype(jnp.bfloat16)
            send(g, 5 + i).start()

    @pl.loop(0, 8)
    def _(g):
        for i, step in enumerate(steps):
            pl.when(g == i)(step)
        zz = z_of(g)

        @pl.loop(0, 4)
        def _(t):
            half = lax.div(t, 2)
            lanes = pl.ds(pl.multiple_of(lax.rem(t, 2) * 256, 256), 256)
            product = lax.dot_general(
                wbuf[zz].reshape(NY * ROWS, KS),
                tokbuf[half, lanes, :],
                (((1,), (1,)), ((), ())),
                preferred_element_type=jnp.float32,
            )
            pbuf[g, :, half, :, lanes] = product.reshape(NY, ROWS, 256).astype(jnp.bfloat16)

        for i in range(5):
            send(g, i).start()
        fin[2, place(zz, c)] = pbuf[g, x, c]

        @pl.when(g > 0)
        def _():
            relay(g - 1)

    relay(7)

    for zz in range(NZ):
        for core in (0, 1):
            for i in (0, 1):
                slot = fin.at[i, place(zz, core)]
                copy(slot, slot, s_x.at[0, 0], r_fin.at[i, zz, core], sibling).wait_recv()
        slot = fin.at[2, place(zz, 1 - c)]
        copy(slot, slot, s_x.at[0, 0], r_sib.at[zz], sibling).wait_recv()

    @pl.loop(0, COLS // HD)
    def _(h):
        rows = pl.ds(pl.multiple_of(h * HD, HD), HD)
        proj = (fin[0, rows].astype(jnp.float32) + fin[1, rows].astype(jnp.float32)) + fin[2, rows].astype(jnp.float32)
        mean_sq = jnp.sum(proj * proj, axis=0, keepdims=True) / HD
        is_qk = x * (COLS // HD) + h < (QR + KR) // HD
        factor = jnp.where(is_qk, 1.0 / jnp.sqrt(mean_sq + norm_eps), 1.0 / math.sqrt(D))
        out[:, rows] = ((proj * factor).T * gain[h]).astype(jnp.bfloat16)

    for sq_send in sq_out:
        sq_send.wait_send()
    tok_out.wait_send()
    for s in SIGNS:
        for hop in (1, 2):
            ay(hop, s).wait_send()
        for k in range(1, 5):
            bz(k, s).wait_send()
            for j in range(4):
                az(k, s, j).wait_send()
        for dz in (0, 1, -1, 2, -2, 3, -3, 4):
            for hop in (1, 2):
                by(dz, hop, s).wait_send()

    @pl.loop(0, 8)
    def _(g):
        for i in range(7):
            send(g, i).wait_send()


def project(tokens, updated, head_gain):
    dma = pltpu.SemaphoreType.DMA
    vmem = pl.BlockSpec(memory_space=pltpu.VMEM)
    bf16 = jnp.bfloat16
    return pl.pallas_call(
        kernel,
        out_shape=(
            jax.ShapeDtypeStruct((TOK, COLS), bf16),
            jax.ShapeDtypeStruct((ROWS, 128), jnp.float32),
        ),
        in_specs=[pl.BlockSpec(memory_space=pl.ANY), vmem, vmem],
        out_specs=(vmem, vmem),
        scratch_shapes=[
            pltpu.VMEM((NZ, NY, ROWS, KS), bf16),
            pltpu.VMEM((2, TOK, KS), bf16),
            pltpu.VMEM((8, NX, 2, ROWS, TOK), bf16),
            pltpu.VMEM((8, 2, ROWS, TOK), bf16),
            pltpu.VMEM((8, 2, ROWS, TOK), bf16),
            pltpu.VMEM((3, COLS, TOK), bf16),
            pltpu.VMEM((NX, ROWS, 128), jnp.float32),
            dma((2, 2)), dma((2, 2)),
            dma((4, 2, 4)), dma((4, 2, 4)),
            dma((4, 2)), dma((4, 2)),
            dma((8, 2, 2)), dma((8, 2, 2)),
            dma((8, 7)), dma((8, 2)), dma((2, NZ, 2)), dma((NZ,)),
            dma((3,)), dma((3,)), dma((3,)),
        ],
        compiler_params=pltpu.CompilerParams(
            collective_id=0, has_side_effects=True, vmem_limit_bytes=48 * 2**20
        ),
        cost_estimate=pl.CostEstimate(
            flops=2 * 2 * TOK * KS * NZ * NY * ROWS, bytes_accessed=4 * 2**20, transcendentals=0
        ),
    )(tokens, updated, head_gain.reshape(COLS // HD, 1, HD))


def body(tokens, qkv_weight, grad, adam_m, adam_v, head_gain):
    new_m = beta_one * adam_m + (1.0 - beta_one) * grad
    new_v = beta_two * adam_v + (1.0 - beta_two) * grad * grad
    updated = qkv_weight - learn_rate * (new_m / bias_one) / (jnp.sqrt(new_v / bias_two) + adam_eps)
    qkv, row_scale = project(tokens, updated, head_gain)
    new_weight = updated * row_scale[:, :1]
    return (new_weight, new_m, new_v, qkv)


def solution(mesh):
    return jax.shard_map(
        body,
        mesh=mesh,
        in_specs=(
            P("dp", "hidden"),
            P("dp", "hidden"),
            P("dp", "hidden"),
            P("dp", "hidden"),
            P("dp", "hidden"),
            P("hidden"),
        ),
        out_specs=(P("dp", "hidden"), P("dp", "hidden"), P("dp", "hidden"), P("dp", "hidden")),
        check_vma=False,
    )
```

time: 416 us -> 109 us (0.26)
  blocking collectives: 251 us -> 0 us
  waiting for transfers between devices: 116 us -> 0 us
  Pallas kernels: 0 us -> 102 us
  matrix products: 16.8 us -> 0 us
  between operations: 14.7 us -> 0.65 us
  other arithmetic: 11.6 us -> 4.27 us
    unnamed x1 -> x0, blocking collectives: 243 us -> none
    all_gather x1 -> x0, waiting for transfers between devices: 116 us -> none  [body(): lax.all_gather(weight_bf, 'dp', axis=0, tiled=True)]
    pallas_call x0 -> x1, Pallas kernels: none -> 102 us  [project(): pl.pallas_call(kernel, out_shape=(jax.ShapeDtypeStruct((TOK, COLS), bf16)...]
    dot_general x1 -> x0, matrix products: 16.8 us -> none  [body(): lax.dot_general(tokens, lax.all_gather(weight_bf, 'dp', axis=0, tiled=Tru...]
    psum x1 -> x0, blocking collectives: 8.4 us -> none  [body(): row_total = lax.psum(partial_value, 'hidden')]
    convert_element_type x2 -> x0, other arithmetic: 5.21 us -> none  [the longest x1 3.24 us: body(): weight_bf = updated.astype(jnp.bfloat16)]
  transfers between devices with their start and end apart: 2 -> 0, of which waited for: 1 -> 0; matrix products, arithmetic and copies ran while one was open for 0% -> 0% of each run, Pallas kernels for 0% -> 0%
where the time goes in v2:
time: 109 us
  Pallas kernels  102 us (94%)
  other arithmetic  4.27 us (4%)
  local copies, waits for them, and re-layouts  1.87 us (2%)
    pallas_call x1, Pallas kernels, project(): pl.pallas_call(kernel, out_shape=(jax.ShapeDtypeStruct((TOK, COLS), bf16)...  102 us
    sub x1, other arithmetic, body(): qkv_weight - learn_rate * (new_m / bias_one) / (jnp.sqrt(new_v / bias_two...  3.31 us

profile of v2, /device:TPU:1, one launch (start us, length us, event | category | flops | bytes accessed | tf_op | source)
XLA Modules:
  0.0 108.8 jit_solution(7193350524482365507)
XLA Ops:
  0.6 0.7 reshape.11.gain
  1.3 0.0 copy-start
  1.3 3.3 %divide_subtract_fusion = (f32[80,2048]{1,0:T(8,128)S(1)}, f32[80,2048]{1,0:T(8,128)}, f32[80,2048]{1,0:T(8,128)}) fusion(f32[80,2048]{1,0:T(8,128)} %param.7, f32[80,2048]{1,0:T(8,128)} %param.8, f32[80,2048]{1,0:T(8,128)} %param.9, f32[80,2048]{1,0:T(8,128)} %param.10), kind=kLoop, calls=%fused_computation.2 | loop fusion | flops 1966080 | bytes 4587520 | tf_op jit(solution)/shard_map/sub | solution.py:370
  4.6 0.0 copy-done
  4.6 102.0 %shard_map.93 = (bf16[512,1280]{1,0:T(8,128)(2,1)S(1)}, f32[80,128]{1,0:T(8,128)S(1)}) custom-call(bf16[512,2048]{1,0:T(8,128)(2,1)S(1)} %copy-done, f32[80,2048]{1,0:T(8,128)S(1)} %get-tuple-element.8.upd, f32[10,1,128]{2,1,0:T(1,128)S(1)} %reshape.11.gain), custom_call_target="tpu_custom_call" | custom-call | flops 10737418240 | bytes 4194304 | tf_op jit(solution)/shard_map/pallas_call | solution.py:335
  106.7 0.1 slice_reduce_fusion
  106.8 1.0 broadcast_multiply_fusion
  107.8 1.1 copy.11
Async XLA Ops:
  1.3 3.3 %copy-start = (bf16[512,2048]{1,0:T(8,128)(2,1)S(1)}, bf16[512,2048]{1,0:T(8,128)(2,1)}, u32[]{:S(2)}) copy-start(bf16[512,2048]{1,0:T(8,128)(2,1)} %tok.1) | copy-start | bytes 6291460

commit v3 on v2

v3 whole, which is shorter than its diff:
```python
import math

import jax
import jax.numpy as jnp
from jax import lax
from jax.experimental import pallas as pl
from jax.experimental.pallas import tpu as pltpu
from jax.sharding import PartitionSpec as P

D = 8192
HD = 128
QR = 4096
KR = 512

NY, NZ, NX = 4, 8, 4
ROWS = 80
SPLIT = 32
KS = 2048
TOK = 512
COLS = 1280
HALF = KS // 2

beta_one = 0.9
beta_two = 0.95
learn_rate = 0.05
adam_eps = 1e-08
norm_eps = 1e-06
bias_one = 0.999973438601112
bias_two = 0.994079470779667

MESH = pl.DeviceIdType.MESH
FIRST, LAST, WHOLE, PAIR = 0, 1, 2, 3
SIGNS = (1, -1)


def side(s):
    return 0 if s > 0 else 1


def group_of(dz):
    if dz == 0:
        return 0
    if dz == 4:
        return 7
    return 2 * dz - 1 if dz > 0 else -2 * dz


def kernel(
    tok, weight, grad, adam_m, adam_v, gain, out, weight_out, m_out, v_out,
    state, wbuf, tokbuf, pbuf, inc, rel, fin, sq,
    s_ay, r_ay, s_az, r_az, s_bz, r_bz, s_by, r_by,
    s_x, r_inc, r_fin, r_sib, s_sq, r_sq, tok_sem, state_sem,
):
    dp = lax.axis_index("dp")
    x = lax.axis_index("hidden")
    y = lax.div(dp, 16)
    z = lax.rem(lax.div(dp, 2), NZ)
    c = lax.rem(dp, 2)

    def device(dy=0, dz=0, dx=0, core=None):
        yy = lax.rem(y + dy + NY, NY)
        zz = lax.rem(z + dz + NZ, NZ)
        return ((yy * NZ + zz) * 2 + (c if core is None else core), lax.rem(x + dx + NX, NX))

    def at_y(dy):
        return lax.rem(y + dy + NY, NY)

    def at_z(dz):
        return lax.rem(z + dz + NZ, NZ)

    def at_x(dx):
        return lax.rem(x + dx + NX, NX)

    y_dev = {s: device(dy=s) for s in SIGNS}
    z_dev = {s: device(dz=s) for s in SIGNS}
    x_dev = {(s, k): device(dx=s, core=k) for s in SIGNS for k in (0, 1)}
    x_two = device(dx=2)
    sibling = device(core=1 - c)

    barrier = pltpu.get_barrier_semaphore()
    partners = list(y_dev.values()) + list(z_dev.values()) + list(x_dev.values()) + [x_two, sibling]
    for partner in partners:
        pl.semaphore_signal(barrier, inc=1, device_id=partner, device_id_type=MESH)

    def copy(src, dst, send_sem, recv_sem, dev):
        return pltpu.make_async_remote_copy(
            src_ref=src, dst_ref=dst, send_sem=send_sem, recv_sem=recv_sem,
            device_id=dev, device_id_type=MESH,
        )

    loads = [
        pltpu.make_async_copy(src, state.at[i], state_sem.at[i])
        for i, src in enumerate((grad, adam_m, adam_v, weight))
    ]
    for load in loads:
        load.start()
    own_tok = pltpu.make_async_copy(tok, tokbuf.at[c], tok_sem.at[0])
    own_tok.start()
    for load in loads:
        load.wait()

    @pl.loop(0, ROWS // 16)
    def _(i):
        rows = pl.ds(pl.multiple_of(i * 16, 16), 16)
        g = state[0, rows]
        new_m = beta_one * state[1, rows] + (1.0 - beta_one) * g
        new_v = beta_two * state[2, rows] + (1.0 - beta_two) * g * g
        updated = state[3, rows] - learn_rate * (new_m / bias_one) / (jnp.sqrt(new_v / bias_two) + adam_eps)
        state[1, rows] = new_m
        state[2, rows] = new_v
        state[3, rows] = updated
        squares = updated * updated
        part = squares[:, 0:128]
        for k in range(1, KS // 128):
            part = part + squares[:, k * 128:(k + 1) * 128]
        sq[x, rows] = part

    pl.semaphore_wait(barrier, len(partners))

    sq_dev = {1: device(dx=1), 2: x_two, 3: device(dx=3)}
    sq_out = [copy(sq.at[x], sq.at[x], s_sq.at[d - 1], r_sq.at[d - 1], sq_dev[d]) for d in (1, 2, 3)]
    for d in (1, 0, 2):
        sq_out[d].start()
    tok_out = copy(tok, tokbuf.at[c], tok_sem.at[1], tok_sem.at[2], sibling)
    tok_out.start()
    for d in (1, 2, 3):
        slot = sq.at[at_x(-d)]
        copy(slot, slot, s_sq.at[d - 1], r_sq.at[d - 1], sibling).wait_recv()
    total = jnp.sum(sq[0] + sq[1] + sq[2] + sq[3], axis=1, keepdims=True)
    row_scale = 1.0 / jnp.sqrt(total / D + norm_eps)
    new_weight = state[3] * row_scale
    wbuf[z, y] = new_weight.astype(jnp.bfloat16)

    def part_a(zz, yy, s=None):
        ref = wbuf.at[zz, yy, pl.ds(0, SPLIT)]
        return ref if s is None else ref.at[:, pl.ds(side(s) * HALF, HALF)]

    def part_b(zz, yy, s=None):
        ref = wbuf.at[zz, yy, pl.ds(SPLIT, ROWS - SPLIT)]
        return ref if s is None else ref.at[:, pl.ds(side(s) * HALF, HALF)]

    y_order = (0, -1, 1, 2)

    def ay(hop, s):
        if hop == 1:
            ref = part_a(z, y)
        else:
            ref = part_a(z, at_y(-s), s)
        return copy(ref, ref, s_ay.at[hop - 1, side(s)], r_ay.at[hop - 1, side(s)], y_dev[s])

    def ay_recv(hop, s):
        ref = part_a(z, at_y(-s)) if hop == 1 else part_a(z, at_y(-2 * s), s)
        copy(ref, ref, s_ay.at[hop - 1, side(s)], r_ay.at[hop - 1, side(s)], y_dev[s]).wait_recv()

    def az(k, s, j):
        ref = part_a(at_z(-(k - 1) * s), at_y(y_order[j]), s if k == 4 else None)
        return copy(ref, ref, s_az.at[k - 1, side(s), j], r_az.at[k - 1, side(s), j], z_dev[s])

    def az_recv(k, s, j):
        ref = part_a(at_z(-k * s), at_y(y_order[j]), s if k == 4 else None)
        copy(ref, ref, s_az.at[k - 1, side(s), j], r_az.at[k - 1, side(s), j], z_dev[s]).wait_recv()

    def bz(k, s):
        ref = part_b(at_z(-(k - 1) * s), y, s if k == 4 else None)
        return copy(ref, ref, s_bz.at[k - 1, side(s)], r_bz.at[k - 1, side(s)], z_dev[s])

    def bz_recv(k, s):
        ref = part_b(at_z(-k * s), y, s if k == 4 else None)
        copy(ref, ref, s_bz.at[k - 1, side(s)], r_bz.at[k - 1, side(s)], z_dev[s]).wait_recv()

    def by(dz, hop, s):
        g = group_of(dz)
        ref = part_b(at_z(-dz), y) if hop == 1 else part_b(at_z(-dz), at_y(-s), s)
        return copy(ref, ref, s_by.at[g, hop - 1, side(s)], r_by.at[g, hop - 1, side(s)], y_dev[s])

    def by_recv(dz, hop, s):
        g = group_of(dz)
        ref = part_b(at_z(-dz), at_y(-s)) if hop == 1 else part_b(at_z(-dz), at_y(-2 * s), s)
        copy(ref, ref, s_by.at[g, hop - 1, side(s)], r_by.at[g, hop - 1, side(s)], y_dev[s]).wait_recv()

    for s in SIGNS:
        ay(1, s).start()
        bz(1, s).start()
    for s in SIGNS:
        by(0, 1, s).start()
        az(1, s, 0).start()

    def pass_z_first(k):
        for s in SIGNS:
            bz_recv(k, s)
            if k < 4:
                bz(k + 1, s).start()

    def start_y(dz):
        for s in SIGNS:
            by(dz, 1, s).start()

    def pass_y(dz):
        for s in SIGNS:
            by_recv(dz, 1, s)
            by(dz, 2, s).start()

    def pass_y_first(k, *js):
        for j in js:
            for s in SIGNS:
                az_recv(k, s, j)
                if k < 4:
                    az(k + 1, s, j).start()

    def arrive(dz):
        for s in SIGNS:
            by_recv(dz, 2, s)

    def open_a():
        for s in SIGNS:
            ay_recv(1, s)
            ay(2, s).start()
        pass_z_first(1)
        for j in (1, 2):
            for s in SIGNS:
                az(1, s, j).start()
        start_y(1)

    def close_a():
        for s in SIGNS:
            ay_recv(2, s)
        for s in SIGNS:
            az(1, s, 3).start()

    pieces = [
        (WHOLE, 0, [open_a, lambda: pass_y(0), lambda: start_y(-1), close_a], [lambda: pass_z_first(2), lambda: arrive(0)]),
        (PAIR, 1, [lambda: pass_y(1), lambda: start_y(2)], [lambda: pass_y_first(1, 0, 1, 2, 3)]),
        (LAST, 1, [lambda: pass_y(-1), lambda: start_y(-2)], [lambda: arrive(1)]),
        (LAST, 2, [lambda: pass_z_first(3), lambda: pass_y(2), lambda: start_y(3)], [lambda: arrive(-1)]),
        (LAST, 3, [lambda: pass_y(-2), lambda: start_y(-3), lambda: pass_y_first(2, 0, 1)], [lambda: arrive(2)]),
        (PAIR, 3, [], [lambda: pass_y_first(2, 2, 3)]),
        (LAST, 4, [lambda: pass_z_first(4), lambda: pass_y(3), lambda: start_y(4)], [lambda: arrive(-2)]),
        (LAST, 5, [lambda: pass_y(-3), lambda: pass_y_first(3, 0, 1)], [lambda: arrive(3)]),
        (PAIR, 5, [], [lambda: pass_y_first(3, 2, 3)]),
        (LAST, 6, [lambda: pass_y(4)], [lambda: arrive(-3)]),
        (WHOLE, 7, [lambda: pass_y_first(4, 0, 1, 2, 3)], [lambda: arrive(4)]),
    ]

    def look_up(p, column):
        value = jnp.int32(pieces[0][column])
        for i in range(1, len(pieces)):
            value = jnp.where(p == i, pieces[i][column], value)
        return value

    def in_turn(p, column):
        for i, piece in enumerate(pieces):
            if piece[column]:
                @pl.when(p == i)
                def _():
                    for act in piece[column]:
                        act()

    def by_kind(p, run):
        kind, g = look_up(p, 0), look_up(p, 1)
        pl.when(kind == WHOLE)(lambda: run([(g, WHOLE)]))
        pl.when(kind == PAIR)(lambda: run([(g, FIRST), (g + 1, FIRST)]))
        pl.when(kind == LAST)(lambda: run([(g, LAST)]))

    state[3] = new_weight
    stores = [
        pltpu.make_async_copy(state.at[i], dst, state_sem.at[i])
        for i, dst in ((1, m_out), (2, v_out), (3, weight_out))
    ]
    for store in stores:
        store.start()
    own_tok.wait()
    copy(tok, tokbuf.at[1 - c], tok_sem.at[1], tok_sem.at[2], sibling).wait_recv()

    def z_of(g):
        dz = jnp.where(lax.rem(g, 2) == 1, lax.div(g + 1, 2), -lax.div(g, 2))
        return lax.rem(z - dz + NZ, NZ)

    starts, lengths = {FIRST: 0, LAST: SPLIT, WHOLE: 0}, {FIRST: SPLIT, LAST: ROWS - SPLIT, WHOLE: ROWS}

    def rows_of(part):
        return pl.ds(starts[part], lengths[part])

    def place(zz, core, part):
        return pl.ds(pl.multiple_of(zz * (2 * ROWS) + core * ROWS + starts[part], 16), lengths[part])

    def send(g, part, i):
        zz = z_of(g)
        rows = rows_of(part)
        here = place(zz, c, part)
        k = part % 2
        src, dst, recv_sem, dev = (
            lambda: (pbuf.at[g, at_x(2), 0, rows], inc.at[g, 0, rows], r_inc.at[g, k, 0], device(dx=-1)),
            lambda: (pbuf.at[g, at_x(2), 1, rows], inc.at[g, 1, rows], r_inc.at[g, k, 1], device(dx=1)),
            lambda: (pbuf.at[g, at_x(-1), 1, rows], fin.at[0, here], r_fin.at[0, g, c, k], x_dev[-1, 1]),
            lambda: (pbuf.at[g, at_x(1), 0, rows], fin.at[1, here], r_fin.at[1, g, c, k], x_dev[1, 0]),
            lambda: (pbuf.at[g, x, 1 - c, rows], fin.at[2, here], r_sib.at[g, k], sibling),
            lambda: (rel.at[g, 0, rows], fin.at[0, here], r_fin.at[0, g, c, k], x_dev[-1, 0]),
            lambda: (rel.at[g, 1, rows], fin.at[1, here], r_fin.at[1, g, c, k], x_dev[1, 1]),
        )[i]()
        return copy(src, dst, s_x.at[g, k, i], recv_sem, dev)

    def multiply(blocks):
        taken = [wbuf[z_of(g), :, rows_of(part)].reshape(-1, KS) for g, part in blocks]
        product = lax.dot_general(
            taken[0] if len(taken) == 1 else jnp.concatenate(taken),
            tokbuf[...].reshape(2 * TOK, KS),
            (((1,), (1,)), ((), ())),
            preferred_element_type=jnp.float32,
        ).astype(jnp.bfloat16)
        for n, (g, part) in enumerate(blocks):
            size = NY * lengths[part]
            for half in (0, 1):
                block = product[n * size:(n + 1) * size, half * TOK:(half + 1) * TOK]
                pbuf[g, :, half, rows_of(part)] = block.reshape(NY, lengths[part], TOK)
        for i in range(5):
            for g, part in blocks:
                send(g, part, i).start()
        for g, part in blocks:
            fin[2, place(z_of(g), c, part)] = pbuf[g, x, c, rows_of(part)]

    def relay(blocks):
        for g, part in blocks:
            rows = rows_of(part)
            for i, owner in ((0, at_x(-1)), (1, at_x(1))):
                send(g, part, i).wait_recv()
                mixed = pbuf[g, owner, i, rows].astype(jnp.float32) + inc[g, i, rows].astype(jnp.float32)
                rel[g, i, rows] = mixed.astype(jnp.bfloat16)
                send(g, part, 5 + i).start()

    @pl.loop(0, len(pieces))
    def _(p):
        in_turn(p, 2)
        in_turn(p, 3)
        by_kind(p, multiply)

        @pl.when(p > 0)
        def _():
            by_kind(p - 1, relay)

    relay([(7, WHOLE)])

    def each_block(run):
        for g in (0, 7):
            run(g, WHOLE)

        @pl.loop(1, 7)
        def _(g):
            run(g, FIRST)
            run(g, LAST)

    def summed(g, part):
        for core in (0, 1):
            for i in (0, 1):
                slot = fin.at[i, place(z_of(g), core, part)]
                copy(slot, slot, s_x.at[0, 0, 0], r_fin.at[i, g, core, part % 2], sibling).wait_recv()
        slot = fin.at[2, place(z_of(g), 1 - c, part)]
        copy(slot, slot, s_x.at[0, 0, 0], r_sib.at[g, part % 2], sibling).wait_recv()

    each_block(summed)

    @pl.loop(0, COLS // HD)
    def _(h):
        rows = pl.ds(pl.multiple_of(h * HD, HD), HD)
        proj = (fin[0, rows].astype(jnp.float32) + fin[1, rows].astype(jnp.float32)) + fin[2, rows].astype(jnp.float32)
        mean_sq = jnp.sum(proj * proj, axis=0, keepdims=True) / HD
        is_qk = x * (COLS // HD) + h < (QR + KR) // HD
        factor = jnp.where(is_qk, 1.0 / jnp.sqrt(mean_sq + norm_eps), 1.0 / math.sqrt(D))
        out[:, rows] = ((proj * factor).T * gain[rows].reshape(1, HD)).astype(jnp.bfloat16)

    for store in stores:
        store.wait()
    for sq_send in sq_out:
        sq_send.wait_send()
    tok_out.wait_send()
    for s in SIGNS:
        for hop in (1, 2):
            ay(hop, s).wait_send()
        for k in range(1, 5):
            bz(k, s).wait_send()
            for j in range(4):
                az(k, s, j).wait_send()
        for dz in (0, 1, -1, 2, -2, 3, -3, 4):
            for hop in (1, 2):
                by(dz, hop, s).wait_send()

    def sent(g, part):
        for i in range(7):
            send(g, part, i).wait_send()

    each_block(sent)


def body(tokens, qkv_weight, grad, adam_m, adam_v, head_gain):
    dma = pltpu.SemaphoreType.DMA
    anywhere = pl.BlockSpec(memory_space=pl.ANY)
    state = jax.ShapeDtypeStruct((ROWS, KS), jnp.float32)
    vmem = pl.BlockSpec(memory_space=pltpu.VMEM)
    bf16 = jnp.bfloat16
    qkv, new_weight, new_m, new_v = pl.pallas_call(
        kernel,
        out_shape=(
            jax.ShapeDtypeStruct((TOK, COLS), bf16),
            state, state, state,
        ),
        in_specs=[pl.BlockSpec(memory_space=pltpu.HBM)] * 5 + [vmem],
        out_specs=(vmem, anywhere, anywhere, anywhere),
        scratch_shapes=[
            pltpu.VMEM((4, ROWS, KS), jnp.float32),
            pltpu.VMEM((NZ, NY, ROWS, KS), bf16),
            pltpu.VMEM((2, TOK, KS), bf16),
            pltpu.VMEM((8, NX, 2, ROWS, TOK), bf16),
            pltpu.VMEM((8, 2, ROWS, TOK), bf16),
            pltpu.VMEM((8, 2, ROWS, TOK), bf16),
            pltpu.VMEM((3, COLS, TOK), bf16),
            pltpu.VMEM((NX, ROWS, 128), jnp.float32),
            dma((2, 2)), dma((2, 2)),
            dma((4, 2, 4)), dma((4, 2, 4)),
            dma((4, 2)), dma((4, 2)),
            dma((8, 2, 2)), dma((8, 2, 2)),
            dma((8, 2, 7)), dma((8, 2, 2)), dma((2, 8, 2, 2)), dma((8, 2)),
            dma((3,)), dma((3,)), dma((3,)), dma((4,)),
        ],
        compiler_params=pltpu.CompilerParams(
            collective_id=0, has_side_effects=True, vmem_limit_bytes=60 * 2**20
        ),
        cost_estimate=pl.CostEstimate(
            flops=2 * 2 * TOK * KS * NZ * NY * ROWS, bytes_accessed=4 * 2**20, transcendentals=0
        ),
    )(tokens, qkv_weight, grad, adam_m, adam_v, head_gain)
    return (new_weight, new_m, new_v, qkv)


def solution(mesh):
    return jax.shard_map(
        body,
        mesh=mesh,
        in_specs=(
            P("dp", "hidden"),
            P("dp", "hidden"),
            P("dp", "hidden"),
            P("dp", "hidden"),
            P("dp", "hidden"),
            P("hidden"),
        ),
        out_specs=(P("dp", "hidden"), P("dp", "hidden"), P("dp", "hidden"), P("dp", "hidden")),
        check_vma=False,
    )
```

time: 109 us -> 96.2 us (0.88)
  Pallas kernels: 102 us -> 90.6 us
  other arithmetic: 4.27 us -> 0 us
  local copies, waits for them, and re-layouts: 1.87 us -> 4.82 us
    pallas_call x1, Pallas kernels: 102 us -> 90.6 us  [body(): pl.pallas_call(kernel, out_shape=(jax.ShapeDtypeStruct((TOK, COLS), bf16)...]
    unnamed x3 -> x10, local copies, waits for them, and re-layouts: 1.06 us -> 4.82 us
    sub x1 -> x0, other arithmetic: 3.31 us -> none  [body(): qkv_weight - learn_rate * (new_m / bias_one) / (jnp.sqrt(new_v / bias_two...]
where the time goes in v3:
time: 96.2 us; the launch traced here: 96 us
  Pallas kernels  90.6 us (94%)
  local copies, waits for them, and re-layouts  4.82 us (5%)
    pallas_call x1, Pallas kernels, body(): pl.pallas_call(kernel, out_shape=(jax.ShapeDtypeStruct((TOK, COLS), bf16)...  90.6 us
    unnamed x10, local copies, waits for them, and re-layouts  4.82 us

profile of v3, /device:TPU:1, one launch (start us, length us, event | category | flops | bytes accessed | tf_op | source)
XLA Modules:
  0.0 96.0 jit_solution(15867016274398927658)
XLA Ops:
  0.6 90.6 %shard_map.93 = (bf16[512,1280]{1,0:T(8,128)(2,1)}, f32[80,2048]{1,0:T(8,128)}, f32[80,2048]{1,0:T(8,128)}, f32[80,2048]{1,0:T(8,128)}) custom-call(bf16[512,2048]{1,0:T(8,128)(2,1)} %tok.1, f32[80,2048]{1,0:T(8,128)} %weight.1, f32[80,2048]{1,0:T(8,128)} %grad.1, f32[80,2048]{1,0:T(8,128)} %adam_m.1, f32[80,2048]{1,0:T(8,128)} %adam_v.1, f32[1280]{0:T(1024)} %gain.1), custom_call_target="tpu_custom_call" | custom-call | flops 10737418240 | bytes 4194304 | tf_op jit(solution)/shard_map/pallas_call | solution.py:399
  91.2 0.0 copy-start.2
  91.2 0.0 copy-start.1
  91.2 2.1 %copy.14 = f32[80,2048]{1,0:T(8,128)} copy(f32[80,2048]{1,0:T(8,128)} %get-tuple-element.16) | data formatting | bytes 1310720
  93.3 0.0 copy-done.2
  93.3 0.0 copy-start
  93.3 0.8 copy.15
  94.1 0.0 copy-done.1
  94.1 0.8 copy.16
  95.0 0.0 copy-done
  95.0 1.1 %copy.17 = bf16[512,1280]{1,0:T(8,128)(2,1)} copy(bf16[512,1280]{1,0:T(8,128)(2,1)S(1)} %copy-done) | data formatting | bytes 2621440
Async XLA Ops:
  91.2 2.1 %copy-start.2 = (f32[80,2048]{1,0:T(8,128)S(1)}, f32[80,2048]{1,0:T(8,128)}, u32[]{:S(2)}) copy-start(f32[80,2048]{1,0:T(8,128)} %get-tuple-element.17) | copy-start | bytes 1966084
  91.2 2.9 %copy-start.1 = (f32[80,2048]{1,0:T(8,128)S(1)}, f32[80,2048]{1,0:T(8,128)}, u32[]{:S(2)}) copy-start(f32[80,2048]{1,0:T(8,128)} %get-tuple-element.18) | copy-start | bytes 1966084
  93.3 1.7 %copy-start = (bf16[512,1280]{1,0:T(8,128)(2,1)S(1)}, bf16[512,1280]{1,0:T(8,128)(2,1)}, u32[]{:S(2)}) copy-start(bf16[512,1280]{1,0:T(8,128)(2,1)} %get-tuple-element.19) | copy-start | bytes 3932164

commit v4 on v3

--- a/solution.py
+++ b/solution.py
@@ -46,10 +46,10 @@
 
 
 def kernel(
-    tok, weight, grad, adam_m, adam_v, gain, out, weight_out, m_out, v_out,
-    state, wbuf, tokbuf, pbuf, inc, rel, fin, sq,
+    tok, weight, grad, adam_m, adam_v, head_gain, out, weight_out, m_out, v_out,
+    state, wbuf, tokbuf, pbuf, inc, rel, fin, sq, pad, near, scales, columns, gain,
     s_ay, r_ay, s_az, r_az, s_bz, r_bz, s_by, r_by,
-    s_x, r_inc, r_fin, r_sib, s_sq, r_sq, tok_sem, state_sem,
+    s_x, r_inc, r_fin, r_sib, s_sq, r_sq, s_near, r_near, s_far, r_far, swap_sem, gain_sem, tok_sem, state_sem,
 ):
     dp = lax.axis_index("dp")
     x = lax.axis_index("hidden")
@@ -79,6 +79,9 @@
 
     barrier = pltpu.get_barrier_semaphore()
     partners = list(y_dev.values()) + list(z_dev.values()) + list(x_dev.values()) + [x_two, sibling]
+    y_two = device(dy=2)
+    z_far = {d: device(dz=d) for d in range(2, NZ - 1)}
+    partners += [y_two] + list(z_far.values())
     for partner in partners:
         pl.semaphore_signal(barrier, inc=1, device_id=partner, device_id_type=MESH)
 
@@ -96,6 +99,8 @@
         load.start()
     own_tok = pltpu.make_async_copy(tok, tokbuf.at[c], tok_sem.at[0])
     own_tok.start()
+    gain_load = pltpu.make_async_copy(head_gain, gain, gain_sem.at[0])
+    gain_load.start()
     for load in loads:
         load.wait()
 
@@ -109,6 +114,7 @@
         state[1, rows] = new_m
         state[2, rows] = new_v
         state[3, rows] = updated
+        wbuf[z, y, rows] = updated.astype(jnp.bfloat16)
         squares = updated * updated
         part = squares[:, 0:128]
         for k in range(1, KS // 128):
@@ -116,20 +122,6 @@
         sq[x, rows] = part
 
     pl.semaphore_wait(barrier, len(partners))
-
-    sq_dev = {1: device(dx=1), 2: x_two, 3: device(dx=3)}
-    sq_out = [copy(sq.at[x], sq.at[x], s_sq.at[d - 1], r_sq.at[d - 1], sq_dev[d]) for d in (1, 2, 3)]
-    for d in (1, 0, 2):
-        sq_out[d].start()
-    tok_out = copy(tok, tokbuf.at[c], tok_sem.at[1], tok_sem.at[2], sibling)
-    tok_out.start()
-    for d in (1, 2, 3):
-        slot = sq.at[at_x(-d)]
-        copy(slot, slot, s_sq.at[d - 1], r_sq.at[d - 1], sibling).wait_recv()
-    total = jnp.sum(sq[0] + sq[1] + sq[2] + sq[3], axis=1, keepdims=True)
-    row_scale = 1.0 / jnp.sqrt(total / D + norm_eps)
-    new_weight = state[3] * row_scale
-    wbuf[z, y] = new_weight.astype(jnp.bfloat16)
 
     def part_a(zz, yy, s=None):
         ref = wbuf.at[zz, yy, pl.ds(0, SPLIT)]
@@ -185,6 +177,72 @@
         by(0, 1, s).start()
         az(1, s, 0).start()
 
+    sq_dev = {1: device(dx=1), 2: x_two, 3: device(dx=3)}
+
+    def sq_copy(d, slot):
+        return copy(sq.at[slot], sq.at[slot], s_sq.at[d - 1], r_sq.at[d - 1], sq_dev[d])
+
+    for d in (2, 1, 3):
+        sq_copy(d, x).start()
+    tok_out = copy(tok, tokbuf.at[c], tok_sem.at[1], tok_sem.at[2], sibling)
+    tok_out.start()
+
+    def stores():
+        return [
+            pltpu.make_async_copy(state.at[i], dst, state_sem.at[i])
+            for i, dst in ((1, m_out), (2, v_out), (3, weight_out))
+        ]
+
+    def scale_rows():
+        for d in (1, 2, 3):
+            sq_copy(d, at_x(-d)).wait_recv()
+        total = jnp.sum(sq[0] + sq[1] + sq[2] + sq[3], axis=1, keepdims=True)
+        row_scale = 1.0 / jnp.sqrt(total / D + norm_eps)
+        pad[...] = jnp.ones_like(pad)
+        pad[0:ROWS] = jnp.broadcast_to(row_scale, (ROWS, 128))
+        near[y] = pad[...].T[0:8]
+        for d in (1, 2, 3):
+            near_copy(d, y).start()
+        state[3] = state[3] * row_scale
+        for store in stores():
+            store.start()
+
+    def near_copy(d, slot):
+        dev = y_two if d == 2 else y_dev[1 if d == 1 else -1]
+        return copy(near.at[slot], near.at[slot], s_near.at[d - 1], r_near.at[d - 1], dev)
+
+    def far_copy(d):
+        dev = z_far[d] if d in z_far else z_dev[1 if d == 1 else -1]
+        return copy(near.at[x], scales.at[c, z], s_far.at[d - 1], r_far.at[d - 1], dev)
+
+    def far_recv(d):
+        slot = scales.at[c, at_z(-d)]
+        copy(slot, slot, s_far.at[d - 1], r_far.at[d - 1], sibling).wait_recv()
+
+    def swap(core):
+        return copy(scales.at[core], scales.at[core], swap_sem.at[0], swap_sem.at[1], sibling)
+
+    def pass_scales():
+        for d in (1, 2, 3):
+            near_copy(d, at_y(-d)).wait_recv()
+        scales[c, z] = near[x]
+        for d in range(1, NZ):
+            far_copy(d).start()
+
+    def swap_scales():
+        for d in range(1, NZ):
+            far_recv(d)
+        swap(c).start()
+
+    def take_scales():
+        swap(1 - c).wait_recv()
+
+        @pl.loop(0, NZ)
+        def _(zz):
+            for core in (0, 1):
+                turned = jnp.broadcast_to(scales[core, zz, 0:1], (128, 128)).T
+                columns[pl.ds(pl.multiple_of(zz * (2 * ROWS) + core * ROWS, 16), ROWS)] = turned[0:ROWS]
+
     def pass_z_first(k):
         for s in SIGNS:
             bz_recv(k, s)
@@ -210,6 +268,11 @@
     def arrive(dz):
         for s in SIGNS:
             by_recv(dz, 2, s)
+
+    def take_tokens():
+        own_tok.wait()
+        gain_load.wait()
+        copy(tok, tokbuf.at[1 - c], tok_sem.at[1], tok_sem.at[2], sibling).wait_recv()
 
     def open_a():
         for s in SIGNS:
@@ -228,15 +291,15 @@
             az(1, s, 3).start()
 
     pieces = [
-        (WHOLE, 0, [open_a, lambda: pass_y(0), lambda: start_y(-1), close_a], [lambda: pass_z_first(2), lambda: arrive(0)]),
+        (WHOLE, 0, [open_a, scale_rows, lambda: pass_y(0), lambda: start_y(-1), close_a], [lambda: pass_z_first(2), take_tokens, lambda: arrive(0)]),
         (PAIR, 1, [lambda: pass_y(1), lambda: start_y(2)], [lambda: pass_y_first(1, 0, 1, 2, 3)]),
         (LAST, 1, [lambda: pass_y(-1), lambda: start_y(-2)], [lambda: arrive(1)]),
-        (LAST, 2, [lambda: pass_z_first(3), lambda: pass_y(2), lambda: start_y(3)], [lambda: arrive(-1)]),
+        (LAST, 2, [lambda: pass_z_first(3), lambda: pass_y(2), lambda: start_y(3), pass_scales], [lambda: arrive(-1)]),
         (LAST, 3, [lambda: pass_y(-2), lambda: start_y(-3), lambda: pass_y_first(2, 0, 1)], [lambda: arrive(2)]),
         (PAIR, 3, [], [lambda: pass_y_first(2, 2, 3)]),
-        (LAST, 4, [lambda: pass_z_first(4), lambda: pass_y(3), lambda: start_y(4)], [lambda: arrive(-2)]),
+        (LAST, 4, [lambda: pass_z_first(4), lambda: pass_y(3), lambda: start_y(4), swap_scales], [lambda: arrive(-2)]),
         (LAST, 5, [lambda: pass_y(-3), lambda: pass_y_first(3, 0, 1)], [lambda: arrive(3)]),
-        (PAIR, 5, [], [lambda: pass_y_first(3, 2, 3)]),
+        (PAIR, 5, [take_scales], [lambda: pass_y_first(3, 2, 3)]),
         (LAST, 6, [lambda: pass_y(4)], [lambda: arrive(-3)]),
         (WHOLE, 7, [lambda: pass_y_first(4, 0, 1, 2, 3)], [lambda: arrive(4)]),
     ]
@@ -260,16 +323,6 @@
         pl.when(kind == WHOLE)(lambda: run([(g, WHOLE)]))
         pl.when(kind == PAIR)(lambda: run([(g, FIRST), (g + 1, FIRST)]))
         pl.when(kind == LAST)(lambda: run([(g, LAST)]))
-
-    state[3] = new_weight
-    stores = [
-        pltpu.make_async_copy(state.at[i], dst, state_sem.at[i])
-        for i, dst in ((1, m_out), (2, v_out), (3, weight_out))
-    ]
-    for store in stores:
-        store.start()
-    own_tok.wait()
-    copy(tok, tokbuf.at[1 - c], tok_sem.at[1], tok_sem.at[2], sibling).wait_recv()
 
     def z_of(g):
         dz = jnp.where(lax.rem(g, 2) == 1, lax.div(g + 1, 2), -lax.div(g, 2))
@@ -337,16 +390,15 @@
         def _():
             by_kind(p - 1, relay)
 
-    relay([(7, WHOLE)])
-
-    def each_block(run):
-        for g in (0, 7):
-            run(g, WHOLE)
-
-        @pl.loop(1, 7)
+    def each_block(first, last, run):
+        @pl.loop(max(first, 1), min(last, 7))
         def _(g):
             run(g, FIRST)
             run(g, LAST)
+
+        for g in (0, 7):
+            if first <= g < last:
+                run(g, WHOLE)
 
     def summed(g, part):
         for core in (0, 1):
@@ -356,21 +408,33 @@
         slot = fin.at[2, place(z_of(g), 1 - c, part)]
         copy(slot, slot, s_x.at[0, 0, 0], r_sib.at[g, part % 2], sibling).wait_recv()
 
-    each_block(summed)
-
-    @pl.loop(0, COLS // HD)
-    def _(h):
+    heads = COLS // HD
+    behind = lax.div(at_z(5) * (2 * ROWS) + HD - 1, HD)
+
+    def finish(i):
+        h = lax.rem(behind + i, heads)
         rows = pl.ds(pl.multiple_of(h * HD, HD), HD)
         proj = (fin[0, rows].astype(jnp.float32) + fin[1, rows].astype(jnp.float32)) + fin[2, rows].astype(jnp.float32)
+        proj = proj * columns[rows, 0:1]
         mean_sq = jnp.sum(proj * proj, axis=0, keepdims=True) / HD
-        is_qk = x * (COLS // HD) + h < (QR + KR) // HD
+        is_qk = x * heads + h < (QR + KR) // HD
         factor = jnp.where(is_qk, 1.0 / jnp.sqrt(mean_sq + norm_eps), 1.0 / math.sqrt(D))
         out[:, rows] = ((proj * factor).T * gain[rows].reshape(1, HD)).astype(jnp.bfloat16)
 
-    for store in stores:
+    each_block(0, 6, summed)
+    pl.loop(0, 6)(finish)
+    relay([(7, WHOLE)])
+    each_block(6, 8, summed)
+    pl.loop(6, heads)(finish)
+
+    for store in stores():
         store.wait()
-    for sq_send in sq_out:
-        sq_send.wait_send()
+    for d in (1, 2, 3):
+        sq_copy(d, x).wait_send()
+        near_copy(d, y).wait_send()
+    for d in range(1, NZ):
+        far_copy(d).wait_send()
+    swap(c).wait_send()
     tok_out.wait_send()
     for s in SIGNS:
         for hop in (1, 2):
@@ -387,7 +451,7 @@
         for i in range(7):
             send(g, part, i).wait_send()
 
-    each_block(sent)
+    each_block(0, 8, sent)
 
 
 def body(tokens, qkv_weight, grad, adam_m, adam_v, head_gain):
@@ -402,7 +466,7 @@
             jax.ShapeDtypeStruct((TOK, COLS), bf16),
             state, state, state,
         ),
-        in_specs=[pl.BlockSpec(memory_space=pltpu.HBM)] * 5 + [vmem],
+        in_specs=[pl.BlockSpec(memory_space=pltpu.HBM)] * 6,
         out_specs=(vmem, anywhere, anywhere, anywhere),
         scratch_shapes=[
             pltpu.VMEM((4, ROWS, KS), jnp.float32),
@@ -413,15 +477,20 @@
             pltpu.VMEM((8, 2, ROWS, TOK), bf16),
             pltpu.VMEM((3, COLS, TOK), bf16),
             pltpu.VMEM((NX, ROWS, 128), jnp.float32),
+            pltpu.VMEM((128, 128), jnp.float32),
+            pltpu.VMEM((NY, 8, 128), jnp.float32),
+            pltpu.VMEM((2, NZ, 8, 128), jnp.float32),
+            pltpu.VMEM((COLS, 128), jnp.float32),
+            pltpu.VMEM((COLS,), jnp.float32),
             dma((2, 2)), dma((2, 2)),
             dma((4, 2, 4)), dma((4, 2, 4)),
             dma((4, 2)), dma((4, 2)),
             dma((8, 2, 2)), dma((8, 2, 2)),
             dma((8, 2, 7)), dma((8, 2, 2)), dma((2, 8, 2, 2)), dma((8, 2)),
-            dma((3,)), dma((3,)), dma((3,)), dma((4,)),
+            dma((3,)), dma((3,)), dma((3,)), dma((3,)), dma((7,)), dma((7,)), dma((2,)), dma((1,)), dma((3,)), dma((4,)),
         ],
         compiler_params=pltpu.CompilerParams(
-            collective_id=0, has_side_effects=True, vmem_limit_bytes=60 * 2**20
+            collective_id=0, has_side_effects=True, vmem_limit_bytes=52 * 2**20
         ),
         cost_estimate=pl.CostEstimate(
             flops=2 * 2 * TOK * KS * NZ * NY * ROWS, bytes_accessed=4 * 2**20, transcendentals=0

time: 96.2 us -> 91.6 us (0.952)
  Pallas kernels: 90.6 us -> 86.6 us
    pallas_call x1, Pallas kernels: 90.6 us -> 86.6 us  [body(): pl.pallas_call(kernel, out_shape=(jax.ShapeDtypeStruct((TOK, COLS), bf16)...]
    unnamed x10 -> x8, local copies, waits for them, and re-layouts: 4.82 us -> 4.26 us
where the time goes in v4:
time: 91.6 us; the launch traced here: 91.5 us
  Pallas kernels  86.6 us (95%)
  local copies, waits for them, and re-layouts  4.26 us (5%)
    pallas_call x1, Pallas kernels, body(): pl.pallas_call(kernel, out_shape=(jax.ShapeDtypeStruct((TOK, COLS), bf16)...  86.6 us
    unnamed x8, local copies, waits for them, and re-layouts  4.26 us

profile of v4, /device:TPU:1, one launch (start us, length us, event | category | flops | bytes accessed | tf_op | source)
XLA Modules:
  0.0 91.5 jit_solution(8012555065398749026)
XLA Ops:
  0.6 0.0 copy-start
  0.6 0.7 copy-done
  1.3 86.6 %shard_map.93 = (bf16[512,1280]{1,0:T(8,128)(2,1)}, f32[80,2048]{1,0:T(8,128)S(1)}, f32[80,2048]{1,0:T(8,128)S(1)}, f32[80,2048]{1,0:T(8,128)S(1)}) custom-call(bf16[512,2048]{1,0:T(8,128)(2,1)} %tok.1, f32[80,2048]{1,0:T(8,128)} %weight.1, f32[80,2048]{1,0:T(8,128)} %grad.1, f32[80,2048]{1,0:T(8,128)} %adam_m.1, f32[80,2048]{1,0:T(8,128)} %adam_v.1, ...), custom_call_target="tpu_custom_call" | custom-call | flops 10737418240 | bytes 4194304 | tf_op jit(solution)/shard_map/pallas_call | solution.py:463
  87.9 0.8 copy.14
  88.8 0.0 copy-start.1
  88.8 0.8 copy.15
  89.6 0.8 copy.16
  90.5 0.0 copy-done.1
  90.5 1.1 %copy.17 = bf16[512,1280]{1,0:T(8,128)(2,1)} copy(bf16[512,1280]{1,0:T(8,128)(2,1)S(1)} %copy-done.1) | data formatting | bytes 2621440
Async XLA Ops:
  0.6 0.7 copy-start
  88.8 1.7 %copy-start.1 = (bf16[512,1280]{1,0:T(8,128)(2,1)S(1)}, bf16[512,1280]{1,0:T(8,128)(2,1)}, u32[]{:S(2)}) copy-start(bf16[512,1280]{1,0:T(8,128)(2,1)} %get-tuple-element.19) | copy-start | bytes 3932164

commit v5 on v4

--- a/solution.py
+++ b/solution.py
@@ -49,7 +49,7 @@
     tok, weight, grad, adam_m, adam_v, head_gain, out, weight_out, m_out, v_out,
     state, wbuf, tokbuf, pbuf, inc, rel, fin, sq, pad, near, scales, columns, gain,
     s_ay, r_ay, s_az, r_az, s_bz, r_bz, s_by, r_by,
-    s_x, r_inc, r_fin, r_sib, s_sq, r_sq, s_near, r_near, s_far, r_far, swap_sem, gain_sem, tok_sem, state_sem,
+    s_x, r_inc, r_fin, r_sib, s_sq, r_sq, s_near, r_near, s_far, r_far, swap_sem, gain_sem, tok_sem, load_sem, state_sem,
 ):
     dp = lax.axis_index("dp")
     x = lax.axis_index("hidden")
@@ -91,26 +91,28 @@
             device_id=dev, device_id_type=MESH,
         )
 
-    loads = [
-        pltpu.make_async_copy(src, state.at[i], state_sem.at[i])
-        for i, src in enumerate((grad, adam_m, adam_v, weight))
-    ]
-    for load in loads:
-        load.start()
+    def load(i, n):
+        rows = pl.ds(pl.multiple_of(i * 16, 16), 16)
+        src = (grad, adam_m, adam_v, weight)[n]
+        return pltpu.make_async_copy(src.at[rows], state.at[n, rows], load_sem.at[i, n])
+
+    for i in range(ROWS // 16):
+        for n in range(4):
+            load(i, n).start()
     own_tok = pltpu.make_async_copy(tok, tokbuf.at[c], tok_sem.at[0])
     own_tok.start()
     gain_load = pltpu.make_async_copy(head_gain, gain, gain_sem.at[0])
     gain_load.start()
-    for load in loads:
-        load.wait()
-
-    @pl.loop(0, ROWS // 16)
-    def _(i):
+
+    def adam(i):
+        for n in range(4):
+            load(i, n).wait()
         rows = pl.ds(pl.multiple_of(i * 16, 16), 16)
         g = state[0, rows]
         new_m = beta_one * state[1, rows] + (1.0 - beta_one) * g
         new_v = beta_two * state[2, rows] + (1.0 - beta_two) * g * g
-        updated = state[3, rows] - learn_rate * (new_m / bias_one) / (jnp.sqrt(new_v / bias_two) + adam_eps)
+        step = (learn_rate / bias_one) * new_m / (jnp.sqrt((1.0 / bias_two) * new_v) + adam_eps)
+        updated = state[3, rows] - step
         state[1, rows] = new_m
         state[2, rows] = new_v
         state[3, rows] = updated
@@ -121,6 +123,7 @@
             part = part + squares[:, k * 128:(k + 1) * 128]
         sq[x, rows] = part
 
+    pl.loop(0, SPLIT // 16)(adam)
     pl.semaphore_wait(barrier, len(partners))
 
     def part_a(zz, yy, s=None):
@@ -172,9 +175,11 @@
 
     for s in SIGNS:
         ay(1, s).start()
+    pl.loop(SPLIT // 16, ROWS // 16)(adam)
+    for s in SIGNS:
         bz(1, s).start()
+        by(0, 1, s).start()
     for s in SIGNS:
-        by(0, 1, s).start()
         az(1, s, 0).start()
 
     sq_dev = {1: device(dx=1), 2: x_two, 3: device(dx=3)}
@@ -354,20 +359,20 @@
 
     def multiply(blocks):
         taken = [wbuf[z_of(g), :, rows_of(part)].reshape(-1, KS) for g, part in blocks]
-        product = lax.dot_general(
-            taken[0] if len(taken) == 1 else jnp.concatenate(taken),
-            tokbuf[...].reshape(2 * TOK, KS),
-            (((1,), (1,)), ((), ())),
-            preferred_element_type=jnp.float32,
-        ).astype(jnp.bfloat16)
-        for n, (g, part) in enumerate(blocks):
-            size = NY * lengths[part]
-            for half in (0, 1):
-                block = product[n * size:(n + 1) * size, half * TOK:(half + 1) * TOK]
+        rows = taken[0] if len(taken) == 1 else jnp.concatenate(taken)
+        for half, sends in ((0, (0, 3)), (1, (1, 2))):
+            product = lax.dot_general(
+                rows, tokbuf[half], (((1,), (1,)), ((), ())), preferred_element_type=jnp.float32
+            ).astype(jnp.bfloat16)
+            for n, (g, part) in enumerate(blocks):
+                size = NY * lengths[part]
+                block = product[n * size:(n + 1) * size]
                 pbuf[g, :, half, rows_of(part)] = block.reshape(NY, lengths[part], TOK)
-        for i in range(5):
-            for g, part in blocks:
-                send(g, part, i).start()
+            for i in sends:
+                for g, part in blocks:
+                    send(g, part, i).start()
+        for g, part in blocks:
+            send(g, part, 4).start()
         for g, part in blocks:
             fin[2, place(z_of(g), c, part)] = pbuf[g, x, c, rows_of(part)]
 
@@ -421,37 +426,39 @@
         factor = jnp.where(is_qk, 1.0 / jnp.sqrt(mean_sq + norm_eps), 1.0 / math.sqrt(D))
         out[:, rows] = ((proj * factor).T * gain[rows].reshape(1, HD)).astype(jnp.bfloat16)
 
+    def sent(g, part):
+        for i in range(7):
+            send(g, part, i).wait_send()
+
+    def sent_before():
+        for store in stores():
+            store.wait()
+        for d in (1, 2, 3):
+            sq_copy(d, x).wait_send()
+            near_copy(d, y).wait_send()
+        for d in range(1, NZ):
+            far_copy(d).wait_send()
+        swap(c).wait_send()
+        tok_out.wait_send()
+        for s in SIGNS:
+            for hop in (1, 2):
+                ay(hop, s).wait_send()
+            for k in range(1, 5):
+                bz(k, s).wait_send()
+                for j in range(4):
+                    az(k, s, j).wait_send()
+            for dz in (0, 1, -1, 2, -2, 3, -3, 4):
+                for hop in (1, 2):
+                    by(dz, hop, s).wait_send()
+        each_block(0, 6, sent)
+
     each_block(0, 6, summed)
     pl.loop(0, 6)(finish)
     relay([(7, WHOLE)])
+    sent_before()
     each_block(6, 8, summed)
     pl.loop(6, heads)(finish)
-
-    for store in stores():
-        store.wait()
-    for d in (1, 2, 3):
-        sq_copy(d, x).wait_send()
-        near_copy(d, y).wait_send()
-    for d in range(1, NZ):
-        far_copy(d).wait_send()
-    swap(c).wait_send()
-    tok_out.wait_send()
-    for s in SIGNS:
-        for hop in (1, 2):
-            ay(hop, s).wait_send()
-        for k in range(1, 5):
-            bz(k, s).wait_send()
-            for j in range(4):
-                az(k, s, j).wait_send()
-        for dz in (0, 1, -1, 2, -2, 3, -3, 4):
-            for hop in (1, 2):
-                by(dz, hop, s).wait_send()
-
-    def sent(g, part):
-        for i in range(7):
-            send(g, part, i).wait_send()
-
-    each_block(0, 8, sent)
+    each_block(6, 8, sent)
 
 
 def body(tokens, qkv_weight, grad, adam_m, adam_v, head_gain):
@@ -487,7 +494,7 @@
             dma((4, 2)), dma((4, 2)),
             dma((8, 2, 2)), dma((8, 2, 2)),
             dma((8, 2, 7)), dma((8, 2, 2)), dma((2, 8, 2, 2)), dma((8, 2)),
-            dma((3,)), dma((3,)), dma((3,)), dma((3,)), dma((7,)), dma((7,)), dma((2,)), dma((1,)), dma((3,)), dma((4,)),
+            dma((3,)), dma((3,)), dma((3,)), dma((3,)), dma((7,)), dma((7,)), dma((2,)), dma((1,)), dma((3,)), dma((ROWS // 16, 4)), dma((4,)),
         ],
         compiler_params=pltpu.CompilerParams(
             collective_id=0, has_side_effects=True, vmem_limit_bytes=52 * 2**20

time: 91.6 us -> 91.4 us (level)
  no operation moved by 1% of the time
where the time goes in v5:
time: 91.4 us; the launch traced here: 91.2 us
  Pallas kernels  86.3 us (94%)
  local copies, waits for them, and re-layouts  4.26 us (5%)
    pallas_call x1, Pallas kernels, body(): pl.pallas_call(kernel, out_shape=(jax.ShapeDtypeStruct((TOK, COLS), bf16)...  86.3 us
    unnamed x8, local copies, waits for them, and re-layouts  4.26 us

profile of v5, /device:TPU:1, one launch (start us, length us, event | category | flops | bytes accessed | tf_op | source)
XLA Modules:
  0.0 91.2 jit_solution(4732048546059698331)
XLA Ops:
  0.6 0.0 copy-start
  0.6 0.7 copy-done
  1.3 86.3 %shard_map.93 = (bf16[512,1280]{1,0:T(8,128)(2,1)}, f32[80,2048]{1,0:T(8,128)S(1)}, f32[80,2048]{1,0:T(8,128)S(1)}, f32[80,2048]{1,0:T(8,128)S(1)}) custom-call(bf16[512,2048]{1,0:T(8,128)(2,1)} %tok.1, f32[80,2048]{1,0:T(8,128)} %weight.1, f32[80,2048]{1,0:T(8,128)} %grad.1, f32[80,2048]{1,0:T(8,128)} %adam_m.1, f32[80,2048]{1,0:T(8,128)} %adam_v.1, ...), custom_call_target="tpu_custom_call" | custom-call | flops 10737418240 | bytes 4194304 | tf_op jit(solution)/shard_map/pallas_call | solution.py:470
  87.7 0.8 copy.14
  88.5 0.0 copy-start.1
  88.5 0.8 copy.15
  89.3 0.8 copy.16
  90.2 0.0 copy-done.1
  90.2 1.1 %copy.17 = bf16[512,1280]{1,0:T(8,128)(2,1)} copy(bf16[512,1280]{1,0:T(8,128)(2,1)S(1)} %copy-done.1) | data formatting | bytes 2621440
Async XLA Ops:
  0.6 0.7 copy-start
  88.5 1.7 %copy-start.1 = (bf16[512,1280]{1,0:T(8,128)(2,1)S(1)}, bf16[512,1280]{1,0:T(8,128)(2,1)}, u32[]{:S(2)}) copy-start(bf16[512,1280]{1,0:T(8,128)(2,1)} %get-tuple-element.19) | copy-start | bytes 3932164

commit v6 on v5

--- a/solution.py
+++ b/solution.py
@@ -296,8 +296,8 @@
             az(1, s, 3).start()
 
     pieces = [
-        (WHOLE, 0, [open_a, scale_rows, lambda: pass_y(0), lambda: start_y(-1), close_a], [lambda: pass_z_first(2), take_tokens, lambda: arrive(0)]),
-        (PAIR, 1, [lambda: pass_y(1), lambda: start_y(2)], [lambda: pass_y_first(1, 0, 1, 2, 3)]),
+        (WHOLE, 0, [open_a, lambda: pass_y(0), lambda: start_y(-1), close_a], [lambda: pass_z_first(2), take_tokens, lambda: arrive(0)]),
+        (PAIR, 1, [lambda: pass_y(1), lambda: start_y(2), scale_rows], [lambda: pass_y_first(1, 0, 1, 2, 3)]),
         (LAST, 1, [lambda: pass_y(-1), lambda: start_y(-2)], [lambda: arrive(1)]),
         (LAST, 2, [lambda: pass_z_first(3), lambda: pass_y(2), lambda: start_y(3), pass_scales], [lambda: arrive(-1)]),
         (LAST, 3, [lambda: pass_y(-2), lambda: start_y(-3), lambda: pass_y_first(2, 0, 1)], [lambda: arrive(2)]),
@@ -360,19 +360,17 @@
     def multiply(blocks):
         taken = [wbuf[z_of(g), :, rows_of(part)].reshape(-1, KS) for g, part in blocks]
         rows = taken[0] if len(taken) == 1 else jnp.concatenate(taken)
-        for half, sends in ((0, (0, 3)), (1, (1, 2))):
-            product = lax.dot_general(
-                rows, tokbuf[half], (((1,), (1,)), ((), ())), preferred_element_type=jnp.float32
-            ).astype(jnp.bfloat16)
-            for n, (g, part) in enumerate(blocks):
-                size = NY * lengths[part]
-                block = product[n * size:(n + 1) * size]
+        product = lax.dot_general(
+            rows, tokbuf[...].reshape(2 * TOK, KS), (((1,), (1,)), ((), ())), preferred_element_type=jnp.float32
+        ).astype(jnp.bfloat16)
+        for n, (g, part) in enumerate(blocks):
+            size = NY * lengths[part]
+            for half in (0, 1):
+                block = product[n * size:(n + 1) * size, half * TOK:(half + 1) * TOK]
                 pbuf[g, :, half, rows_of(part)] = block.reshape(NY, lengths[part], TOK)
-            for i in sends:
-                for g, part in blocks:
-                    send(g, part, i).start()
-        for g, part in blocks:
-            send(g, part, 4).start()
+        for i in range(5):
+            for g, part in blocks:
+                send(g, part, i).start()
         for g, part in blocks:
             fin[2, place(z_of(g), c, part)] = pbuf[g, x, c, rows_of(part)]
 
@@ -459,6 +457,31 @@
     each_block(6, 8, summed)
     pl.loop(6, heads)(finish)
     each_block(6, 8, sent)
+
+
+def hand_over_kernel(*refs):
+    results, outputs, held, load_sem, store_sem = refs[0:4], refs[4:8], refs[8:12], refs[12], refs[13]
+    loads = [pltpu.make_async_copy(results[i], held[i], load_sem.at[i]) for i in range(4)]
+    stores = [pltpu.make_async_copy(held[i], outputs[i], store_sem.at[i]) for i in range(4)]
+    for load in loads:
+        load.start()
+    for load, store in zip(loads, stores):
+        load.wait()
+        store.start()
+    for store in stores:
+        store.wait()
+
+
+def hand_over(*arrays):
+    return pl.pallas_call(
+        hand_over_kernel,
+        out_shape=[jax.ShapeDtypeStruct(a.shape, a.dtype) for a in arrays],
+        in_specs=[pl.BlockSpec(memory_space=pl.ANY)] * 4,
+        out_specs=[pl.BlockSpec(memory_space=pl.ANY)] * 4,
+        scratch_shapes=[pltpu.VMEM(a.shape, a.dtype) for a in arrays]
+        + [pltpu.SemaphoreType.DMA((4,)), pltpu.SemaphoreType.DMA((4,))],
+        compiler_params=pltpu.CompilerParams(vmem_limit_bytes=60 * 2**20),
+    )(*arrays)
 
 
 def body(tokens, qkv_weight, grad, adam_m, adam_v, head_gain):
@@ -497,13 +520,13 @@
             dma((3,)), dma((3,)), dma((3,)), dma((3,)), dma((7,)), dma((7,)), dma((2,)), dma((1,)), dma((3,)), dma((ROWS // 16, 4)), dma((4,)),
         ],
         compiler_params=pltpu.CompilerParams(
-            collective_id=0, has_side_effects=True, vmem_limit_bytes=52 * 2**20
+            collective_id=0, has_side_effects=True, vmem_limit_bytes=60 * 2**20
         ),
         cost_estimate=pl.CostEstimate(
             flops=2 * 2 * TOK * KS * NZ * NY * ROWS, bytes_accessed=4 * 2**20, transcendentals=0
         ),
     )(tokens, qkv_weight, grad, adam_m, adam_v, head_gain)
-    return (new_weight, new_m, new_v, qkv)
+    return hand_over(new_weight, new_m, new_v, qkv)
 
 
 def solution(mesh):

time: 91.4 us -> 90.2 us (0.987)
  local copies, waits for them, and re-layouts: 4.26 us -> 0 us
  Pallas kernels: 86.3 us -> 89.5 us
    unnamed x8 -> x0, local copies, waits for them, and re-layouts: 4.26 us -> none
    pallas_call x0 -> x1, Pallas kernels: none -> 3.04 us  [hand_over(): pl.pallas_call(hand_over_kernel, out_shape=[jax.ShapeDtypeStruct(a.shape,...]
where the time goes in v6:
time: 90.2 us; the launch traced here: 90.1 us
  Pallas kernels  89.5 us (99%)
    pallas_call x1, Pallas kernels, body(): pl.pallas_call(kernel, out_shape=(jax.ShapeDtypeStruct((TOK, COLS), bf16)...  86.4 us
    pallas_call x1, Pallas kernels, hand_over(): pl.pallas_call(hand_over_kernel, out_shape=[jax.ShapeDtypeStruct(a.shape,...  3.04 us

profile of v6, /device:TPU:1, one launch (start us, length us, event | category | flops | bytes accessed | tf_op | source)
XLA Modules:
  0.0 90.1 jit_solution(15162520559886427325)
XLA Ops:
  0.6 86.4 %shard_map.93 = (bf16[512,1280]{1,0:T(8,128)(2,1)}, f32[80,2048]{1,0:T(8,128)}, f32[80,2048]{1,0:T(8,128)}, f32[80,2048]{1,0:T(8,128)}) custom-call(bf16[512,2048]{1,0:T(8,128)(2,1)} %tok.1, f32[80,2048]{1,0:T(8,128)} %weight.1, f32[80,2048]{1,0:T(8,128)} %grad.1, f32[80,2048]{1,0:T(8,128)} %adam_m.1, f32[80,2048]{1,0:T(8,128)} %adam_v.1, f32[1280]{0:T(1024)} %head_gain.1), custom_call_target="tpu_custom_call" | custom-call | flops 10737418240 | bytes 4194304 | tf_op jit(solution)/shard_map/pallas_call | solution.py:493
  87.1 3.0 %shard_map.94 = (f32[80,2048]{1,0:T(8,128)}, f32[80,2048]{1,0:T(8,128)}, f32[80,2048]{1,0:T(8,128)}, bf16[512,1280]{1,0:T(8,128)(2,1)}) custom-call(f32[80,2048]{1,0:T(8,128)} %get-tuple-element.8.refs_0_, f32[80,2048]{1,0:T(8,128)} %get-tuple-element.9.refs_1_, f32[80,2048]{1,0:T(8,128)} %get-tuple-element.10.refs_2_, ...), custom_call_target="tpu_custom_call" | custom-call | tf_op jit(solution)/shard_map/pallas_call | solution.py:476

commit v7 on v6

--- a/solution.py
+++ b/solution.py
@@ -46,10 +46,10 @@
 
 
 def kernel(
-    tok, weight, grad, adam_m, adam_v, head_gain, out, weight_out, m_out, v_out,
-    state, wbuf, tokbuf, pbuf, inc, rel, fin, sq, pad, near, scales, columns, gain,
+    tok, weight, grad, adam_m, adam_v, head_gain, qkv_out, weight_out, m_out, v_out,
+    state, wbuf, tokbuf, pbuf, inc, rel, fin, sq, pad, near, scales, columns, gain, out,
     s_ay, r_ay, s_az, r_az, s_bz, r_bz, s_by, r_by,
-    s_x, r_inc, r_fin, r_sib, s_sq, r_sq, s_near, r_near, s_far, r_far, swap_sem, gain_sem, tok_sem, load_sem, state_sem,
+    s_x, r_inc, r_fin, r_sib, s_sq, r_sq, s_near, r_near, s_far, r_far, swap_sem, gain_sem, out_sem, tok_sem, load_sem, state_sem,
 ):
     dp = lax.axis_index("dp")
     x = lax.axis_index("hidden")
@@ -414,6 +414,11 @@
     heads = COLS // HD
     behind = lax.div(at_z(5) * (2 * ROWS) + HD - 1, HD)
 
+    def leave(i):
+        h = lax.rem(behind + i, heads)
+        rows = pl.ds(pl.multiple_of(h * HD, HD), HD)
+        return pltpu.make_async_copy(out.at[:, rows], qkv_out.at[:, rows], out_sem.at[i])
+
     def finish(i):
         h = lax.rem(behind + i, heads)
         rows = pl.ds(pl.multiple_of(h * HD, HD), HD)
@@ -423,6 +428,7 @@
         is_qk = x * heads + h < (QR + KR) // HD
         factor = jnp.where(is_qk, 1.0 / jnp.sqrt(mean_sq + norm_eps), 1.0 / math.sqrt(D))
         out[:, rows] = ((proj * factor).T * gain[rows].reshape(1, HD)).astype(jnp.bfloat16)
+        leave(i).start()
 
     def sent(g, part):
         for i in range(7):
@@ -458,11 +464,19 @@
     pl.loop(6, heads)(finish)
     each_block(6, 8, sent)
 
+    @pl.loop(0, heads)
+    def _(i):
+        leave(i).wait()
+
 
 def hand_over_kernel(*refs):
     results, outputs, held, load_sem, store_sem = refs[0:4], refs[4:8], refs[8:12], refs[12], refs[13]
-    loads = [pltpu.make_async_copy(results[i], held[i], load_sem.at[i]) for i in range(4)]
-    stores = [pltpu.make_async_copy(held[i], outputs[i], store_sem.at[i]) for i in range(4)]
+    blocks = []
+    for i in range(4):
+        size = results[i].shape[0] // 5 if i < 3 else results[i].shape[0] // 4
+        blocks += [(i, n, pl.ds(n * size, size)) for n in range(5 if i < 3 else 4)]
+    loads = [pltpu.make_async_copy(results[i].at[r], held[i].at[r], load_sem.at[i, n]) for i, n, r in blocks]
+    stores = [pltpu.make_async_copy(held[i].at[r], outputs[i].at[r], store_sem.at[i, n]) for i, n, r in blocks]
     for load in loads:
         load.start()
     for load, store in zip(loads, stores):
@@ -479,7 +493,7 @@
         in_specs=[pl.BlockSpec(memory_space=pl.ANY)] * 4,
         out_specs=[pl.BlockSpec(memory_space=pl.ANY)] * 4,
         scratch_shapes=[pltpu.VMEM(a.shape, a.dtype) for a in arrays]
-        + [pltpu.SemaphoreType.DMA((4,)), pltpu.SemaphoreType.DMA((4,))],
+        + [pltpu.SemaphoreType.DMA((4, 5)), pltpu.SemaphoreType.DMA((4, 5))],
         compiler_params=pltpu.CompilerParams(vmem_limit_bytes=60 * 2**20),
     )(*arrays)
 
@@ -488,7 +502,6 @@
     dma = pltpu.SemaphoreType.DMA
     anywhere = pl.BlockSpec(memory_space=pl.ANY)
     state = jax.ShapeDtypeStruct((ROWS, KS), jnp.float32)
-    vmem = pl.BlockSpec(memory_space=pltpu.VMEM)
     bf16 = jnp.bfloat16
     qkv, new_weight, new_m, new_v = pl.pallas_call(
         kernel,
@@ -497,7 +510,7 @@
             state, state, state,
         ),
         in_specs=[pl.BlockSpec(memory_space=pltpu.HBM)] * 6,
-        out_specs=(vmem, anywhere, anywhere, anywhere),
+        out_specs=[anywhere] * 4,
         scratch_shapes=[
             pltpu.VMEM((4, ROWS, KS), jnp.float32),
             pltpu.VMEM((NZ, NY, ROWS, KS), bf16),
@@ -512,12 +525,13 @@
             pltpu.VMEM((2, NZ, 8, 128), jnp.float32),
             pltpu.VMEM((COLS, 128), jnp.float32),
             pltpu.VMEM((COLS,), jnp.float32),
+            pltpu.VMEM((TOK, COLS), bf16),
             dma((2, 2)), dma((2, 2)),
             dma((4, 2, 4)), dma((4, 2, 4)),
             dma((4, 2)), dma((4, 2)),
             dma((8, 2, 2)), dma((8, 2, 2)),
             dma((8, 2, 7)), dma((8, 2, 2)), dma((2, 8, 2, 2)), dma((8, 2)),
-            dma((3,)), dma((3,)), dma((3,)), dma((3,)), dma((7,)), dma((7,)), dma((2,)), dma((1,)), dma((3,)), dma((ROWS // 16, 4)), dma((4,)),
+            dma((3,)), dma((3,)), dma((3,)), dma((3,)), dma((7,)), dma((7,)), dma((2,)), dma((1,)), dma((COLS // HD,)), dma((3,)), dma((ROWS // 16, 4)), dma((4,)),
         ],
         compiler_params=pltpu.CompilerParams(
             collective_id=0, has_side_effects=True, vmem_limit_bytes=60 * 2**20

time: 90.2 us -> 90.3 us (level)
  no operation moved by 1% of the time
where the time goes in v7:
time: 90.3 us; the launch traced here: 90.2 us
  Pallas kernels  89.5 us (99%)
    pallas_call x1, Pallas kernels, body(): pl.pallas_call(kernel, out_shape=(jax.ShapeDtypeStruct((TOK, COLS), bf16)...  86.1 us
    pallas_call x1, Pallas kernels, hand_over(): pl.pallas_call(hand_over_kernel, out_shape=[jax.ShapeDtypeStruct(a.shape,...  3.45 us

profile of v7, /device:TPU:1, one launch (start us, length us, event | category | flops | bytes accessed | tf_op | source)
XLA Modules:
  0.0 90.2 jit_solution(9487155402080702205)
XLA Ops:
  0.6 86.1 %shard_map.93 = (bf16[512,1280]{1,0:T(8,128)(2,1)}, f32[80,2048]{1,0:T(8,128)}, f32[80,2048]{1,0:T(8,128)}, f32[80,2048]{1,0:T(8,128)}) custom-call(bf16[512,2048]{1,0:T(8,128)(2,1)} %tok.1, f32[80,2048]{1,0:T(8,128)} %weight.1, f32[80,2048]{1,0:T(8,128)} %grad.1, f32[80,2048]{1,0:T(8,128)} %adam_m.1, f32[80,2048]{1,0:T(8,128)} %adam_v.1, f32[1280]{0:T(1024)} %head_gain.1), custom_call_target="tpu_custom_call" | custom-call | flops 10737418240 | bytes 4194304 | tf_op jit(solution)/shard_map/pallas_call | solution.py:506
  86.7 3.4 %shard_map.94 = (f32[80,2048]{1,0:T(8,128)}, f32[80,2048]{1,0:T(8,128)}, f32[80,2048]{1,0:T(8,128)}, bf16[512,1280]{1,0:T(8,128)(2,1)}) custom-call(f32[80,2048]{1,0:T(8,128)} %get-tuple-element.8.refs_0_, f32[80,2048]{1,0:T(8,128)} %get-tuple-element.9.refs_1_, f32[80,2048]{1,0:T(8,128)} %get-tuple-element.10.refs_2_, ...), custom_call_target="tpu_custom_call" | custom-call | tf_op jit(solution)/shard_map/pallas_call | solution.py:490
